TPU v7x, 128 devices: a whole 4x4x4 slice. The times are simulated.
128 devices in a mesh: fsdp: 32 (over z, x, core), seq: 4 (over y).
Axes of the slice: x: 4, y: 4, z: 4, core: 2. Of those that a mesh axis runs over, the one named last changes fastest.
Arguments:
- tokens: bfloat16 [49152, 768], P(('fsdp', 'seq')), may hold values from -24 to 24
- slot_seq: int32 [384], P('fsdp'), may hold values from 0 to 2, as said below
- slot_block_index: int32 [384], P('fsdp'), may hold values from 0 to 7
- lengths: int32 [32, 3], P('fsdp'), may hold values from 1 to 1024, as said below
- ln1_gain: bfloat16 [768], P(('fsdp', 'seq')), may hold values from 0.25 to 1.75
- ln1_bias: bfloat16 [768], P(('fsdp', 'seq')), may hold values from -1.75 to 1.75
- w_qkv: bfloat16 [768, 2304], P(('fsdp', 'seq')), may hold values from -0.21875 to 0.21875
- qv_bias: bfloat16 [1536], P(('fsdp', 'seq')), may hold values from -0.625 to 0.625
- w_out: bfloat16 [768, 768], P(('fsdp', 'seq')), may hold values from -1.75 to 1.75
- out_bias: bfloat16 [768], P(('fsdp', 'seq')), may hold values from -1.75 to 1.75
- ln2_gain: bfloat16 [768], P(('fsdp', 'seq')), may hold values from 0.25 to 1.75
- ln2_bias: bfloat16 [768], P(('fsdp', 'seq')), may hold values from -1.75 to 1.75
- w_fc: bfloat16 [768, 3072], P(('fsdp', 'seq')), may hold values from -0.21875 to 0.21875
- feed_input_bias: bfloat16 [3072], P(('fsdp', 'seq')), may hold values from -3 to 3
- w_proj: bfloat16 [3072, 768], P(('fsdp', 'seq')), may hold values from -0.109375 to 0.109375
- proj_bias: bfloat16 [768], P(('fsdp', 'seq')), may hold values from -1.75 to 1.75
- cotangent: bfloat16 [49152, 768], P(('fsdp', 'seq')), may hold values from -6 to 6
Outputs:
- block_out: bfloat16 [49152, 768], P(('fsdp', 'seq'))
- tokens_grad: bfloat16 [49152, 768], P(('fsdp', 'seq'))
- ln1_gain_grad: float32 [768], P(('fsdp', 'seq'))
- ln1_bias_grad: float32 [768], P(('fsdp', 'seq'))
- w_qkv_grad: float32 [768, 2304], P(('fsdp', 'seq'))
- qv_bias_grad: float32 [1536], P(('fsdp', 'seq'))
- w_out_grad: float32 [768, 768], P(('fsdp', 'seq'))
- out_bias_grad: float32 [768], P(('fsdp', 'seq'))
- ln2_gain_grad: float32 [768], P(('fsdp', 'seq'))
- ln2_bias_grad: float32 [768], P(('fsdp', 'seq'))
- w_fc_grad: float32 [768, 3072], P(('fsdp', 'seq'))
- fc_bias_grad: float32 [3072], P(('fsdp', 'seq'))
- w_proj_grad: float32 [3072, 768], P(('fsdp', 'seq'))
- proj_bias_grad: float32 [768], P(('fsdp', 'seq'))
Inputs may be any that keep to these rules, and one draw needn't show every extreme that they name: `slot_seq`: in each group every slot holds one block of one sequence; block b of a sequence covers its positions b * 128 to b * 128 + 127, and a sequence of length L has exactly (L + 127) // 128 blocks in its group, each in one slot. `lengths`: one sequence of each group has length 1024.
All inputs are finite; a program needn't handle non-finite values.
Results may differ from a plain program's by a relative error of at most 0.019.
Values may be sent and summed in bfloat16 or wider, within the bound.
No kernel may reach another device: no remote copies, remote signals or barrier semaphores. Data moves between devices by JAX's collectives and lax.ppermute only.
A program may use at most 128 MiB of HBM per device.

v0:
```python
import jax
import jax.numpy as jnp
from jax import lax
from jax.sharding import PartitionSpec as P

D = 768
H = 12
HD = 64
BLK = 128


EPSILON = 1e-05
MASKED_SCORE = -1e30


def normalized_rows(value, gain, shift):
    center = jnp.mean(value, axis=-1, keepdims=True)
    offset = value - center
    spread = jnp.mean(offset * offset, axis=-1, keepdims=True)
    return offset * lax.rsqrt(spread + EPSILON) * gain + shift


def gelu_tanh(value):
    return jax.nn.gelu(value, approximate=True)


def pair_heads(value):
    return jnp.transpose(value.reshape(value.shape[0], H // 2, 2 * HD), (1, 0, 2))


def unpair_heads(value):
    return jnp.transpose(value, (1, 0, 2)).reshape(value.shape[1], D)


def on_device(
    tokens,
    slot_seq,
    slot_block_index,
    lengths,
    ln1_gain,
    ln1_bias,
    w_qkv,
    qv_bias,
    w_out,
    out_bias,
    ln2_gain,
    ln2_bias,
    w_fc,
    feed_input_bias,
    w_proj,
    proj_bias,
    cotangent,
):
    row_count = tokens.shape[0]
    group_slots = slot_seq.shape[0]
    key_count = group_slots * BLK
    score_scale = HD ** (-0.5)
    shards = (
        ln1_gain,
        ln1_bias,
        w_qkv,
        qv_bias,
        w_out,
        out_bias,
        ln2_gain,
        ln2_bias,
        w_fc,
        feed_input_bias,
        w_proj,
        proj_bias,
    )
    gathered = (
        lax.all_gather(shards[0], ("fsdp", "seq"), axis=0, tiled=True),
        lax.all_gather(shards[1], ("fsdp", "seq"), axis=0, tiled=True),
        lax.all_gather(shards[2], ("fsdp", "seq"), axis=0, tiled=True),
        lax.all_gather(shards[3], ("fsdp", "seq"), axis=0, tiled=True),
        lax.all_gather(shards[4], ("fsdp", "seq"), axis=0, tiled=True),
        lax.all_gather(shards[5], ("fsdp", "seq"), axis=0, tiled=True),
        lax.all_gather(shards[6], ("fsdp", "seq"), axis=0, tiled=True),
        lax.all_gather(shards[7], ("fsdp", "seq"), axis=0, tiled=True),
        lax.all_gather(shards[8], ("fsdp", "seq"), axis=0, tiled=True),
        lax.all_gather(shards[9], ("fsdp", "seq"), axis=0, tiled=True),
        lax.all_gather(shards[10], ("fsdp", "seq"), axis=0, tiled=True),
        lax.all_gather(shards[11], ("fsdp", "seq"), axis=0, tiled=True),
    )
    (
        gain_one,
        shift_one,
        joined_weight,
        joined_bias,
        out_weight,
        out_shift,
        gain_two,
        shift_two,
        fc_weight,
        fc_shift,
        proj_weight,
        proj_shift,
    ) = gathered
    offsets = lax.broadcasted_iota(jnp.int32, (group_slots, BLK), 1)
    key_seq = jnp.broadcast_to(slot_seq[:, None], (group_slots, BLK)).reshape(key_count)
    key_pos = (slot_block_index[:, None] * BLK + offsets).reshape(key_count)
    seq_ids = lax.broadcasted_iota(jnp.int32, (key_count, lengths.shape[1]), 1)
    key_len = jnp.sum(jnp.where(key_seq[:, None] == seq_ids, lengths, 0), axis=1)
    start_row = lax.axis_index("seq") * row_count
    row_seq = lax.dynamic_slice_in_dim(key_seq, start_row, row_count)
    row_pos = lax.dynamic_slice_in_dim(key_pos, start_row, row_count)
    row_len = lax.dynamic_slice_in_dim(key_len, start_row, row_count)
    visible = (
        (row_seq[:, None] == key_seq[None, :])
        & (key_pos[None, :] <= row_pos[:, None])
        & (key_pos[None, :] < key_len[None, :])
    )
    live = (row_pos < row_len).astype(jnp.float32)
    inputs = tokens.astype(jnp.float32)
    normed_one, pull_one = jax.vjp(
        normalized_rows, inputs, gain_one.astype(jnp.float32), shift_one.astype(jnp.float32)
    )
    acts_one = normed_one.astype(jnp.bfloat16)
    joined = jnp.dot(acts_one, joined_weight, preferred_element_type=jnp.float32)
    bias_wide = joined_bias.astype(jnp.float32)
    queries = (joined[:, :D] + bias_wide[:D]).astype(jnp.bfloat16)
    key_rows = joined[:, D : 2 * D].astype(jnp.bfloat16)
    value_rows = (joined[:, 2 * D :] + bias_wide[D:]).astype(jnp.bfloat16)
    key_all, value_all = (
        lax.all_gather(key_rows, "seq", axis=0, tiled=True),
        lax.all_gather(value_rows, "seq", axis=0, tiled=True),
    )
    query_pairs = pair_heads(queries)
    key_pairs = pair_heads(key_all)
    value_pairs = pair_heads(value_all)

    def pair_scores(query_pair, key_pair):
        scores = (
            jnp.einsum(
                "qhd,khd->hqk",
                query_pair.reshape(row_count, 2, HD),
                key_pair.reshape(key_count, 2, HD),
                preferred_element_type=jnp.float32,
            )
            * score_scale
        )
        return jnp.where(visible[None], scores, MASKED_SCORE)

    def attend_pair(pieces):
        query_pair, key_pair, value_pair = pieces
        scores = pair_scores(query_pair, key_pair)
        top_score = jnp.max(scores, axis=-1, keepdims=True)
        weights = jnp.exp(scores - top_score)
        total = jnp.sum(weights, axis=-1, keepdims=True)
        probs = weights / total
        mixed = jnp.einsum(
            "hqk,khd->qhd",
            probs.astype(jnp.bfloat16),
            value_pair.reshape(key_count, 2, HD),
            preferred_element_type=jnp.float32,
        )
        return (mixed.reshape(row_count, 2 * HD), (top_score + jnp.log(total))[..., 0])

    mixed_pairs, log_totals = lax.map(attend_pair, (query_pairs, key_pairs, value_pairs))
    mixed = unpair_heads(mixed_pairs).astype(jnp.bfloat16)
    middle = (
        inputs
        + jnp.dot(mixed, out_weight, preferred_element_type=jnp.float32)
        + out_shift.astype(jnp.float32)
    )
    normed_two, pull_two = jax.vjp(
        normalized_rows, middle, gain_two.astype(jnp.float32), shift_two.astype(jnp.float32)
    )
    acts_two = normed_two.astype(jnp.bfloat16)
    hidden = jnp.dot(acts_two, fc_weight, preferred_element_type=jnp.float32) + fc_shift.astype(
        jnp.float32
    )
    gelu_value, gelu_pull = jax.vjp(gelu_tanh, hidden)
    active = gelu_value.astype(jnp.bfloat16)
    result = (
        middle
        + jnp.dot(active, proj_weight, preferred_element_type=jnp.float32)
        + proj_shift.astype(jnp.float32)
    )
    block_out = result.astype(jnp.bfloat16)
    again = (
        lax.all_gather(shards[0], ("fsdp", "seq"), axis=0, tiled=True),
        lax.all_gather(shards[1], ("fsdp", "seq"), axis=0, tiled=True),
        lax.all_gather(shards[2], ("fsdp", "seq"), axis=0, tiled=True),
        lax.all_gather(shards[3], ("fsdp", "seq"), axis=0, tiled=True),
        lax.all_gather(shards[4], ("fsdp", "seq"), axis=0, tiled=True),
        lax.all_gather(shards[5], ("fsdp", "seq"), axis=0, tiled=True),
        lax.all_gather(shards[6], ("fsdp", "seq"), axis=0, tiled=True),
        lax.all_gather(shards[7], ("fsdp", "seq"), axis=0, tiled=True),
        lax.all_gather(shards[8], ("fsdp", "seq"), axis=0, tiled=True),
        lax.all_gather(shards[9], ("fsdp", "seq"), axis=0, tiled=True),
        lax.all_gather(shards[10], ("fsdp", "seq"), axis=0, tiled=True),
        lax.all_gather(shards[11], ("fsdp", "seq"), axis=0, tiled=True),
    )
    joined_back = again[2]
    out_back = again[4]
    fc_back = again[8]
    proj_back = again[10]
    out_grad = (cotangent.astype(jnp.float32) * live[:, None]).astype(jnp.bfloat16)
    grad_proj = jnp.einsum("rf,rd->fd", active, out_grad, preferred_element_type=jnp.float32)
    grad_proj_bias = jnp.sum(out_grad.astype(jnp.float32), axis=0)
    active_grad = jnp.einsum("rd,fd->rf", out_grad, proj_back, preferred_element_type=jnp.float32)
    hidden_grad = gelu_pull(active_grad)[0].astype(jnp.bfloat16)
    grad_fc = jnp.einsum("rd,rf->df", acts_two, hidden_grad, preferred_element_type=jnp.float32)
    grad_fc_bias = jnp.sum(hidden_grad.astype(jnp.float32), axis=0)
    acts_two_grad = jnp.einsum(
        "rf,df->rd", hidden_grad, fc_back, preferred_element_type=jnp.float32
    )
    middle_norm_grad, grad_ln2_gain, grad_ln2_bias = pull_two(acts_two_grad)
    middle_grad = out_grad.astype(jnp.float32) + middle_norm_grad
    attn_grad = middle_grad.astype(jnp.bfloat16)
    grad_out = jnp.einsum("rc,rd->cd", mixed, attn_grad, preferred_element_type=jnp.float32)
    grad_out_bias = jnp.sum(attn_grad.astype(jnp.float32), axis=0)
    mixed_grad = jnp.einsum(
        "rd,cd->rc", attn_grad, out_back, preferred_element_type=jnp.float32
    ).astype(jnp.bfloat16)
    mixed_grad_pairs = pair_heads(mixed_grad)

    def attend_back(pieces):
        query_pair, key_pair, value_pair, grad_pair, log_total = pieces
        scores = pair_scores(query_pair, key_pair)
        probs = jnp.exp(scores - log_total[..., None])
        query_two = query_pair.reshape(row_count, 2, HD)
        grad_two = grad_pair.reshape(row_count, 2, HD)
        prob_grad = jnp.einsum(
            "qhd,khd->hqk",
            grad_two,
            value_pair.reshape(key_count, 2, HD),
            preferred_element_type=jnp.float32,
        )
        row_dot = jnp.sum(prob_grad * probs, axis=-1, keepdims=True)
        score_grad = (probs * (prob_grad - row_dot)).astype(jnp.bfloat16)
        query_grad = (
            jnp.einsum(
                "hqk,khd->qhd",
                score_grad,
                key_pair.reshape(key_count, 2, HD),
                preferred_element_type=jnp.float32,
            )
            * score_scale
        )
        key_grad = (
            jnp.einsum("hqk,qhd->khd", score_grad, query_two, preferred_element_type=jnp.float32)
            * score_scale
        )
        value_grad = jnp.einsum(
            "hqk,qhd->khd", probs.astype(jnp.bfloat16), grad_two, preferred_element_type=jnp.float32
        )
        return (
            query_grad.reshape(row_count, 2 * HD),
            key_grad.reshape(key_count, 2 * HD),
            value_grad.reshape(key_count, 2 * HD),
        )

    query_grad_pairs, key_grad_pairs, value_grad_pairs = lax.map(
        attend_back, (query_pairs, key_pairs, value_pairs, mixed_grad_pairs, log_totals)
    )
    key_own, value_own = (
        lax.psum_scatter(
            unpair_heads(key_grad_pairs).astype(jnp.bfloat16),
            "seq",
            scatter_dimension=0,
            tiled=True,
        ).astype(jnp.float32),
        lax.psum_scatter(
            unpair_heads(value_grad_pairs).astype(jnp.bfloat16),
            "seq",
            scatter_dimension=0,
            tiled=True,
        ).astype(jnp.float32),
    )
    query_grad = unpair_heads(query_grad_pairs).astype(jnp.bfloat16)
    value_grad = value_own.astype(jnp.bfloat16)
    joined_grad = jnp.concatenate([query_grad, key_own.astype(jnp.bfloat16), value_grad], axis=1)
    grad_qkv = jnp.einsum("rc,re->ce", acts_one, joined_grad, preferred_element_type=jnp.float32)
    grad_qv_bias = jnp.concatenate(
        [
            jnp.sum(query_grad.astype(jnp.float32), axis=0),
            jnp.sum(value_grad.astype(jnp.float32), axis=0),
        ]
    )
    acts_one_grad = jnp.einsum(
        "re,ce->rc", joined_grad, joined_back, preferred_element_type=jnp.float32
    )
    input_norm_grad, grad_ln1_gain, grad_ln1_bias = pull_one(acts_one_grad)
    tokens_grad = (middle_grad + input_norm_grad).astype(jnp.bfloat16)
    local_grads = (
        grad_ln1_gain,
        grad_ln1_bias,
        grad_qkv,
        grad_qv_bias,
        grad_out,
        grad_out_bias,
        grad_ln2_gain,
        grad_ln2_bias,
        grad_fc,
        grad_fc_bias,
        grad_proj,
        grad_proj_bias,
    )
    owned = (
        lax.psum_scatter(local_grads[0], ("fsdp", "seq"), scatter_dimension=0, tiled=True),
        lax.psum_scatter(local_grads[1], ("fsdp", "seq"), scatter_dimension=0, tiled=True),
        lax.psum_scatter(local_grads[2], ("fsdp", "seq"), scatter_dimension=0, tiled=True),
        lax.psum_scatter(local_grads[3], ("fsdp", "seq"), scatter_dimension=0, tiled=True),
        lax.psum_scatter(local_grads[4], ("fsdp", "seq"), scatter_dimension=0, tiled=True),
        lax.psum_scatter(local_grads[5], ("fsdp", "seq"), scatter_dimension=0, tiled=True),
        lax.psum_scatter(local_grads[6], ("fsdp", "seq"), scatter_dimension=0, tiled=True),
        lax.psum_scatter(local_grads[7], ("fsdp", "seq"), scatter_dimension=0, tiled=True),
        lax.psum_scatter(local_grads[8], ("fsdp", "seq"), scatter_dimension=0, tiled=True),
        lax.psum_scatter(local_grads[9], ("fsdp", "seq"), scatter_dimension=0, tiled=True),
        lax.psum_scatter(local_grads[10], ("fsdp", "seq"), scatter_dimension=0, tiled=True),
        lax.psum_scatter(local_grads[11], ("fsdp", "seq"), scatter_dimension=0, tiled=True),
    )
    return (
        block_out,
        tokens_grad,
        owned[0],
        owned[1],
        owned[2],
        owned[3],
        owned[4],
        owned[5],
        owned[6],
        owned[7],
        owned[8],
        owned[9],
        owned[10],
        owned[11],
    )


def solution(mesh):
    in_specs = (
        P(("fsdp", "seq"), None),
        P("fsdp"),
        P("fsdp"),
        P("fsdp", None),
        P(("fsdp", "seq")),
        P(("fsdp", "seq")),
        P(("fsdp", "seq"), None),
        P(("fsdp", "seq")),
        P(("fsdp", "seq"), None),
        P(("fsdp", "seq")),
        P(("fsdp", "seq")),
        P(("fsdp", "seq")),
        P(("fsdp", "seq"), None),
        P(("fsdp", "seq")),
        P(("fsdp", "seq"), None),
        P(("fsdp", "seq")),
        P(("fsdp", "seq"), None),
    )
    out_specs = (
        P(("fsdp", "seq"), None),
        P(("fsdp", "seq"), None),
        P(("fsdp", "seq")),
        P(("fsdp", "seq")),
        P(("fsdp", "seq"), None),
        P(("fsdp", "seq")),
        P(("fsdp", "seq"), None),
        P(("fsdp", "seq")),
        P(("fsdp", "seq")),
        P(("fsdp", "seq")),
        P(("fsdp", "seq"), None),
        P(("fsdp", "seq")),
        P(("fsdp", "seq"), None),
        P(("fsdp", "seq")),
    )
    return jax.shard_map(
        on_device, mesh=mesh, in_specs=in_specs, out_specs=out_specs, check_vma=False
    )
```

profile of v0, /device:TPU:0, one launch (start us, length us, event | category | flops | bytes accessed | tf_op | source)
XLA Modules:
  0.0 1339.7 jit_solution(9581532510331148965)
XLA Ops:
  16.2 70.0 %all-reduce.23 = (bf16[768]{0:T(1024)(128)(2,1)S(1)}, bf16[768]{0:T(1024)(128)(2,1)S(1)}, bf16[1536]{0:T(1024)(128)(2,1)S(1)}, bf16[768]{0:T(1024)(128)(2,1)S(1)...) all-reduce(bf16[768]{0:T(1024)(128)(2,1)S(1)} %dynamic-update-slice, ...), channel_id=1, replica_groups=mesh['fsdp'=32,'seq'=4] {'fsdp','seq'}, use_global_device_ids=true, to_apply=%add.1 | all-reduce | flops 9216 | bytes 36864
  89.4 6.7 reshape.247
  110.6 34.6 %all-gather.18.cloned.1.call-done = bf16[128,6,768]{2,1,0:T(8,128)(2,1)} async-done(((bf16[1,6,768]{2,1,0:T(8,128)(2,1)}), bf16[128,6,768]{2,1,0:T(8,128)(2,1)}) %all-gather.18.cloned.1.call-update) | async-done | bytes 1179664 | tf_op jit(solution)/shard_map/all_gather | solution.py:77
  148.6 65.1 %all-gather.20.cloned.1.call-done = bf16[128,6,3072]{2,1,0:T(8,128)(2,1)} async-done(((bf16[1,6,3072]{2,1,0:T(8,128)(2,1)}), bf16[128,6,3072]{2,1,0:T(8,128)(2,1)}) %all-gather.20.cloned.1.call-update) | async-done | bytes 4718608 | tf_op jit(solution)/shard_map/all_gather | solution.py:81
  213.8 7.7 reshape.251
  221.5 25.1 %all-gather.10.cloned.1.call-done = bf16[1536,768]{1,0:T(8,128)(2,1)} async-done(((bf16[384,768]{1,0:T(8,128)(2,1)}), bf16[1536,768]{1,0:T(8,128)(2,1)}) %all-gather.10.cloned.1.call-update) | async-done | bytes 2359312 | tf_op jit(solution)/shard_map/all_gather | solution.py:127
  249.4 32.4 %all-gather.12.cloned.1.call-done = bf16[1536,768]{1,0:T(8,128)(2,1)} async-done(((bf16[384,768]{1,0:T(8,128)(2,1)}), bf16[1536,768]{1,0:T(8,128)(2,1)}) %all-gather.12.cloned.1.call-update) | async-done | bytes 2359312 | tf_op jit(solution)/shard_map/all_gather | solution.py:126
  286.9 46.8 %while.28 = (s32[]{:T(128)}, bf16[6,384,128]{1,2,0:T(8,128)(2,1)}, f32[6,2,384]{2,1,0:T(2,128)}, bf16[6,1536,128]{1,2,0:T(8,128)(2,1)S(1)}, bf16[6,384,128]{1,2,...) while((s32[]{:T(128)}, bf16[6,384,128]{1,2,0:T(8,128)(2,1)}, ...), condition=%wide.region_6.7_spmd.clone, body=%wide.region_3.6_spmd.clone.sunk | while | flops 318504192 | bytes 19505804 | solution.py:160
  338.1 6.8 convolution_add_fusion
  344.9 6.9 all-gather.14.cloned.1.call-done
  351.8 9.0 convert_reduce_fusion
  371.9 63.2 %while.29 = (s32[]{:T(128)}, bf16[6,384,128]{1,2,0:T(8,128)(2,1)S(1)}, bf16[6,1536,128]{1,2,0:T(8,128)(2,1)}, bf16[6,1536,128]{1,2,0:T(8,128)(2,1)}, bf16[6,1536...) while((s32[]{:T(128)}, ...), condition=%wide.region_13.14_spmd.clone, body=%wide.region_11.13_spmd.clone.sunk | while | flops 768441600 | bytes 42794672 | solution.py:256
  444.6 9.4 fusion.51
  470.3 32.6 %reduce-scatter.16.cloned.1.call-done = bf16[384,768]{1,0:T(8,128)(2,1)} async-done(((bf16[1536,768]{1,0:T(8,128)(2,1)}), bf16[384,768]{1,0:T(8,128)(2,1)}) %reduce-scatter.16.cloned.1.call-update) | async-done | bytes 589840
  505.0 6.2 fusion.38
  511.2 373.1 %fusion.54 = (f32[8,2304]{1,0:T(8,128)}, f32[8,768]{1,0:T(8,128)}, f32[8,3072]{1,0:T(8,128)}) fusion(f32[768,2304]{1,0:T(8,128)} %fusion.38, f32[768,768]{1,0:T(8,128)} %fusion.59, f32[768,3072]{1,0:T(8,128)} %fusion.50), kind=kCustom, calls=%all-reduce-scatter.3 | all-reduce-scatter fusion | flops 6291457 | bytes 19070976
  896.9 16.0 %collective-permute-start.54 = (f32[8,768]{1,0:T(8,128)}, f32[8,768]{1,0:T(8,128)S(1)}, u32[]{:S(2)}, u32[]{:S(2)}) collective-permute-start(f32[8,768]{1,0:T(8,128)} %get-tuple-element.252), channel_id=1, source_target_pairs={{0,23},{1,24},{2,25},{3,26},{4,27},{5,28},{6,29},{7,30},{8,31},{9,... | collective-permute-start | bytes 73736
  1013.0 7.4 fusion.29
  1089.2 7.3 collective-permute-start.87
  1129.2 7.6 collective-permute-start.74
  1136.9 63.6 %all-reduce.22 = (f32[768]{0:T(1024)S(1)}, f32[768]{0:T(1024)S(1)}, f32[1536]{0:T(1024)S(1)}, f32[768]{0:T(1024)S(1)}, f32[768]{0:T(1024)S(1)}, /*index=5*/f32[7...) all-reduce(f32[768]{0:T(1024)} %get-tuple-element.177, ...), channel_id=4, replica_groups=mesh['fsdp'=32,'seq'=4] {'fsdp','seq'}, use_global_device_ids=true, to_apply=%region_19.20.clone | all-reduce | flops 9216 | bytes 73728
  1205.1 27.2 %concatenate.9 = f32[262,768]{1,0:T(8,128)S(1)} concatenate(f32[6,768]{1,0:T(8,128)} %copy-done.84, f32[8,768]{1,0:T(8,128)} %copy-done.82, f32[8,768]{1,0:T(8,128)} %copy-done.83, f32[8,768]{1,0:T(8,128)} %copy-done.85, f32[8,768]{1,0:T(8,128)} %copy-done.86, f32[8,768]{1,0:T(8,128)} %copy-done.87, f32[8,768]{1,0:T(8,128)} %copy-done.88, f32[8,768]{1,0:T(8,128)} %copy-done.89, ...), dimensions={0} | concatenate | bytes 1609728
  1250.8 32.6 %concatenate.8 = f32[262,2304]{1,0:T(8,128)S(1)} concatenate(f32[6,2304]{1,0:T(8,128)} %copy-done.55, f32[8,2304]{1,0:T(8,128)} %collective-permute-done.30, f32[8,2304]{1,0:T(8,128)} %collective-permute-done.29, f32[8,2304]{1,0:T(8,128)} %collective-permute-done.28, f32[8,2304]{1,0:T(8,128)} %collective-permute-done.27, f32[8,2304]{1,0:T(8,128)} %collective-permute-done.26, ...), dimensions={0} | concatenate | bytes 4829184
  1300.8 31.5 %concatenate.10 = f32[262,3072]{1,0:T(8,128)S(1)} concatenate(f32[6,3072]{1,0:T(8,128)S(1)} %collective-permute-done.95, f32[8,3072]{1,0:T(8,128)S(1)} %collective-permute-done.94, f32[8,3072]{1,0:T(8,128)S(1)} %collective-permute-done.93, f32[8,3072]{1,0:T(8,128)} %copy-done.34, f32[8,3072]{1,0:T(8,128)} %copy-done.35, f32[8,3072]{1,0:T(8,128)} %collective-permute-done.90, ...), dimensions={0} | concatenate | bytes 6438912
  (681 shorter events, 443.8 us)
Async XLA Ops:
  7.2 82.2 %all-gather.16.cloned.1.call-start = ((), (), s32[]{:S(2)}) async-start(), calls=%async_computation.7 | async-start | bytes 4755456 | tf_op jit(solution)/shard_map/all_gather | solution.py:75
  7.9 137.2 %all-gather.18.cloned.1.call-start = ((), (), s32[]{:S(2)}) async-start(), calls=%async_computation.8 | async-start | bytes 1585152 | tf_op jit(solution)/shard_map/all_gather | solution.py:77
  8.7 205.1 %all-gather.20.cloned.1.call-start = ((), (), s32[]{:S(2)}) async-start(), calls=%async_computation.9 | async-start | bytes 6340608 | tf_op jit(solution)/shard_map/all_gather | solution.py:81
  9.4 237.2 %all-gather.10.cloned.1.call-start = ((), (), s32[]{:S(2)}) async-start(), calls=%async_computation.3 | async-start | bytes 2949120 | tf_op jit(solution)/shard_map/all_gather | solution.py:127
  102.6 179.2 %all-gather.12.cloned.1.call-start = ((), (), s32[]{:S(2)}) async-start(), calls=%async_computation.4 | async-start | bytes 2949120 | tf_op jit(solution)/shard_map/all_gather | solution.py:126
  104.8 247.0 %all-gather.14.cloned.1.call-start = ((), (), s32[]{:S(2)}) async-start(), calls=%async_computation.5 | async-start | bytes 4755456 | tf_op jit(solution)/shard_map/all_gather | solution.py:83
  105.4 363.5 %reduce-scatter.18.cloned.1.call-start = ((), (), s32[]{:S(2)}) async-start(), calls=%async_computation.11 | async-start | bytes 2949120
  439.4 63.4 %reduce-scatter.16.cloned.1.call-start = ((), (), s32[]{:S(2)}) async-start(), calls=%async_computation.10 | async-start | bytes 2949120
  443.6 889.4 %reduce-scatter.14.cloned.1.call-start = ((), (), s32[]{:S(2)}) async-start(), calls=%async_computation.6 | async-start | bytes 9510912 | tf_op jit(solution)/shard_map/reduce_scatter | solution.py:313
  896.9 23.6 %collective-permute-start.54 = (f32[8,768]{1,0:T(8,128)}, f32[8,768]{1,0:T(8,128)S(1)}, u32[]{:S(2)}, u32[]{:S(2)}) collective-permute-start(f32[8,768]{1,0:T(8,128)} %get-tuple-element.252), channel_id=1, source_target_pairs={{0,23},{1,24},{2,25},{3,26},{4,27},{5,28},{6,29},{7,30},{8,31},{9,... | collective-permute-start | bytes 73736
  965.3 26.0 %collective-permute-start.30 = (f32[8,2304]{1,0:T(8,128)}, f32[8,2304]{1,0:T(8,128)}, u32[]{:S(2)}, u32[]{:S(2)}) collective-permute-start(f32[8,2304]{1,0:T(8,128)} %get-tuple-element.251), channel_id=1, source_target_pairs={{0,31},{1,32},{2,33},{3,34},{4,35},{5,36},{6,37},{7,38},{8,39},{9,... | collective-permute-start | bytes 221192
  967.2 26.9 %collective-permute-start.29 = (f32[8,2304]{1,0:T(8,128)}, f32[8,2304]{1,0:T(8,128)}, u32[]{:S(2)}, u32[]{:S(2)}) collective-permute-start(f32[8,2304]{1,0:T(8,128)} %get-tuple-element.251), channel_id=1, source_target_pairs={{0,30},{1,31},{2,32},{3,33},{4,34},{5,35},{6,36},{7,37},{8,38},{9,... | collective-permute-start | bytes 221192
  970.0 26.0 %collective-permute-start.28 = (f32[8,2304]{1,0:T(8,128)}, f32[8,2304]{1,0:T(8,128)}, u32[]{:S(2)}, u32[]{:S(2)}) collective-permute-start(f32[8,2304]{1,0:T(8,128)} %get-tuple-element.251), channel_id=1, source_target_pairs={{0,29},{1,30},{2,31},{3,32},{4,33},{5,34},{6,35},{7,36},{8,37},{9,... | collective-permute-start | bytes 221192
  1002.5 23.6 %collective-permute-start.20 = (f32[8,2304]{1,0:T(8,128)}, f32[8,2304]{1,0:T(8,128)S(1)}, u32[]{:S(2)}, u32[]{:S(2)}) collective-permute-start(f32[8,2304]{1,0:T(8,128)} %get-tuple-element.251), channel_id=1, source_target_pairs={{0,21},{1,22},{2,23},{3,24},{4,25},{5,26},{6,27},{7,28},{8,29},{9,... | collective-permute-start | bytes 221192
  1119.2 113.2 %collective-permute-start.78 = (f32[8,3072]{1,0:T(8,128)}, f32[8,3072]{1,0:T(8,128)S(1)}, u32[]{:S(2)}, u32[]{:S(2)}) collective-permute-start(f32[8,3072]{1,0:T(8,128)} %get-tuple-element.253), channel_id=1, source_target_pairs={{0,15},{1,16},{2,17},{3,18},{4,19},{5,20},{6,21},{7,22},{8,23},{9,... | collective-permute-start | bytes 294920
  1121.6 113.4 %collective-permute-start.77 = (f32[8,3072]{1,0:T(8,128)}, f32[8,3072]{1,0:T(8,128)S(1)}, u32[]{:S(2)}, u32[]{:S(2)}) collective-permute-start(f32[8,3072]{1,0:T(8,128)} %get-tuple-element.253), channel_id=1, source_target_pairs={{0,14},{1,15},{2,16},{3,17},{4,18},{5,19},{6,20},{7,21},{8,22},{9,... | collective-permute-start | bytes 294920
  1124.8 114.6 %collective-permute-start.76 = (f32[8,3072]{1,0:T(8,128)}, f32[8,3072]{1,0:T(8,128)S(1)}, u32[]{:S(2)}, u32[]{:S(2)}) collective-permute-start(f32[8,3072]{1,0:T(8,128)} %get-tuple-element.253), channel_id=1, source_target_pairs={{0,13},{1,14},{2,15},{3,16},{4,17},{5,18},{6,19},{7,20},{8,21},{9,... | collective-permute-start | bytes 294920
  1127.3 116.0 %collective-permute-start.75 = (f32[8,3072]{1,0:T(8,128)}, f32[8,3072]{1,0:T(8,128)S(1)}, u32[]{:S(2)}, u32[]{:S(2)}) collective-permute-start(f32[8,3072]{1,0:T(8,128)} %get-tuple-element.253), channel_id=1, source_target_pairs={{0,12},{1,13},{2,14},{3,15},{4,16},{5,17},{6,18},{7,19},{8,20},{9,... | collective-permute-start | bytes 294920
  1129.2 117.9 %collective-permute-start.74 = (f32[8,3072]{1,0:T(8,128)}, f32[8,3072]{1,0:T(8,128)S(1)}, u32[]{:S(2)}, u32[]{:S(2)}) collective-permute-start(f32[8,3072]{1,0:T(8,128)} %get-tuple-element.253), channel_id=1, source_target_pairs={{0,11},{1,12},{2,13},{3,14},{4,15},{5,16},{6,17},{7,18},{8,19},{9,... | collective-permute-start | bytes 294920
  1232.3 51.1 %collective-permute-start.73 = (f32[8,3072]{1,0:T(8,128)}, f32[8,3072]{1,0:T(8,128)}, u32[]{:S(2)}, u32[]{:S(2)}) collective-permute-start(f32[8,3072]{1,0:T(8,128)} %get-tuple-element.253), channel_id=1, source_target_pairs={{0,10},{1,11},{2,12},{3,13},{4,14},{5,15},{6,16},{7,17},{8,18},{9,... | collective-permute-start | bytes 294920
  1235.0 50.1 %collective-permute-start.72 = (f32[8,3072]{1,0:T(8,128)}, f32[8,3072]{1,0:T(8,128)}, u32[]{:S(2)}, u32[]{:S(2)}) collective-permute-start(f32[8,3072]{1,0:T(8,128)} %get-tuple-element.253), channel_id=1, source_target_pairs={{0,9},{1,10},{2,11},{3,12},{4,13},{5,14},{6,15},{7,16},{8,17},{9,1... | collective-permute-start | bytes 294920
  1239.4 48.5 %collective-permute-start.71 = (f32[8,3072]{1,0:T(8,128)}, f32[8,3072]{1,0:T(8,128)}, u32[]{:S(2)}, u32[]{:S(2)}) collective-permute-start(f32[8,3072]{1,0:T(8,128)} %get-tuple-element.253), channel_id=1, source_target_pairs={{0,8},{1,9},{2,10},{3,11},{4,12},{5,13},{6,14},{7,15},{8,16},{9,17... | collective-permute-start | bytes 294920
  1243.3 48.2 %collective-permute-start.70 = (f32[8,3072]{1,0:T(8,128)}, f32[8,3072]{1,0:T(8,128)}, u32[]{:S(2)}, u32[]{:S(2)}) collective-permute-start(f32[8,3072]{1,0:T(8,128)} %get-tuple-element.253), channel_id=1, source_target_pairs={{0,7},{1,8},{2,9},{3,10},{4,11},{5,12},{6,13},{7,14},{8,15},{9,16}... | collective-permute-start | bytes 294920
  1247.1 47.8 %collective-permute-start.69 = (f32[8,3072]{1,0:T(8,128)}, f32[8,3072]{1,0:T(8,128)}, u32[]{:S(2)}, u32[]{:S(2)}) collective-permute-start(f32[8,3072]{1,0:T(8,128)} %get-tuple-element.253), channel_id=1, source_target_pairs={{0,6},{1,7},{2,8},{3,9},{4,10},{5,11},{6,12},{7,13},{8,14},{9,15},... | collective-permute-start | bytes 294920
  (208 other events, 4634.0 us)
Sparse Core Ops, SparseCore 0:
  11.0 69.4 all-gather.15
  83.3 61.7 all-gather.17
  148.1 65.5 all-gather.19
  215.9 30.6 all-gather.9
  248.7 33.0 all-gather.11
  284.6 67.1 all-gather.13
  439.5 29.2 reduce-scatter.17
  471.3 31.5 reduce-scatter.15
  508.5 232.4 reduce-scatter.13
where the time goes:
time: 1360 us; the launch traced here: 1340 us
  blocking collectives  507 us (37%)
  starting transfers between devices  262 us (19%)
  waiting for transfers between devices  208 us (15%)
  local copies, waits for them, and re-layouts  197 us (14%)
  matrix products  104 us (8%)
  other arithmetic  43.9 us (3%)
  between operations  16.7 us (1%)
    unnamed x3, blocking collectives  507 us
    unnamed x98, starting transfers between devices  262 us
    unnamed x294, local copies, waits for them, and re-layouts  147 us
    all_gather x1, waiting for transfers between devices, on_device(): lax.all_gather(shards[8], ('fsdp', 'seq'), axis=0, tiled=True)  65.1 us
    unnamed x107, waiting for transfers between devices  44 us
    all_gather x1, waiting for transfers between devices, on_device(): lax.all_gather(shards[4], ('fsdp', 'seq'), axis=0, tiled=True)  34.6 us
    all_gather x1, waiting for transfers between devices, on_device(): lax.all_gather(key_rows, 'seq', axis=0, tiled=True)  32.4 us
  transfers between devices with their start and end apart: 105, of which 10 were waited for; matrix products, arithmetic and copies ran while one was open for 46% of the time, Pallas kernels for 0%

commit v1 on v0

v1 whole, which is shorter than its diff:
```python
import numpy as np
import jax
import jax.numpy as jnp
from jax import lax
from jax.experimental import pallas as pl
from jax.experimental.pallas import tpu as pltpu
from jax.sharding import PartitionSpec as P

D = 768
H = 12
HD = 64
FF = 3072
BLK = 128
SLOTS = 3
NY = 4
GSLOTS = SLOTS * NY
ROWS = SLOTS * BLK
GROWS = GSLOTS * BLK
LONG = 8
LONG_LEN = LONG * BLK
HEADS = H // NY
HW = HEADS * HD
WQ = 3 * HW
QCOLS = 640
C_FC = 768
C_PROJ = C_FC + FF
C_VEC = C_PROJ + FF
WCOLS = C_VEC + 128
EPSILON = 1e-05
MASKED_SCORE = -1e30
SCALE = HD**-0.5
SEQ_STRIDE = 4096
M_INV, M_CODE, M_BASE, M_LIM, M_ZXY, M_THR = 0, 12, 16, 20, 24, 27
F32 = jnp.float32
BF16 = jnp.bfloat16
TILES = tuple((256 * t, 0, 256 * (t + 1)) for t in range(4)) + ((1024, 1024, 256), (1280, 1024, 512))


def dot_nn(a, b):
    return lax.dot_general(a, b, (((1,), (0,)), ((), ())), preferred_element_type=F32)


def dot_nt(a, b):
    return lax.dot_general(a, b, (((1,), (1,)), ((), ())), preferred_element_type=F32)


def dot_tn(a, b):
    return lax.dot_general(a, b, (((0,), (0,)), ((), ())), preferred_element_type=F32)


def normed(value):
    center = jnp.mean(value, axis=-1, keepdims=True)
    offset = value - center
    spread = jnp.mean(offset * offset, axis=-1, keepdims=True)
    scale = lax.rsqrt(spread + EPSILON)
    return offset * scale, scale


def minus(a, k, n):
    r = a - k
    return jnp.where(r < 0, r + n, r)


def visible_mask(meta, tile):
    q0, k0, count = tile
    row = lax.broadcasted_iota(jnp.int32, (256, 1), 0)
    col = lax.broadcasted_iota(jnp.int32, (1, count), 1)
    if q0 < LONG_LEN:
        return col <= row + q0
    first = (q0 - LONG_LEN) // BLK

    def per_slot(base, index, start, n):
        value = jnp.full(index.shape, meta[base + start], jnp.int32)
        for i in range(1, n):
            value = jnp.where(index >= i * BLK, meta[base + start + i], value)
        return value

    q_code = per_slot(M_CODE, row, first, 2) + (row & (BLK - 1))
    q_base = per_slot(M_BASE, row, first, 2)
    slots = count // BLK
    k_code = per_slot(M_CODE, col, 0, slots) + (col & (BLK - 1))
    k_lim = per_slot(M_LIM, col, 0, slots)
    k_code = jnp.where(k_code < k_lim, k_code, 1 << 24)
    return (k_code <= q_code) & (k_code >= q_base)


def select_matrix(r0, offset):
    rows = lax.broadcasted_iota(jnp.int32, (D, HW), 0)
    return jnp.where(rows == r0 + offset, 1.0, 0.0).astype(BF16)


def front_kernel(nz, nx, meta, *refs):
    x_refs, refs = refs[:NY], refs[NY:]
    z_refs, refs = refs[:nz], refs[nz:]
    r0_ref, k_ref = refs[:2]
    a1_ref, qkv_ref, lse_ref = refs[2:5]
    o_refs = refs[5 : 5 + NY]
    w_ref, gain_ref, oh = refs[5 + NY :]
    z, x, y = meta[M_ZXY], meta[M_ZXY + 1], meta[M_ZXY + 2]
    step = D // (nz * nx)
    for kz in range(nz):
        for kx in range(nx):
            at = (minus(z, kz, nz) * nx + minus(x, kx, nx)) * step
            w_ref[pl.ds(pl.multiple_of(at, step), step), :] = z_refs[kz][kx]
    vectors = jnp.transpose(w_ref[:, 512:640].astype(F32))
    gain = vectors[64:65]
    shift = vectors[65:66]
    gain_ref[...] = jnp.broadcast_to(gain, (8, D))
    small = vectors[64:72].astype(BF16)
    odd = k_ref[...] == 1
    sums = dot_nn(small, select_matrix(r0_ref[...], 96 * y))
    q_bias = jnp.where(odd, sums[3:4], sums[2:3])
    sums = dot_nn(small, select_matrix(r0_ref[...], 384 + 96 * y))
    v_bias = jnp.where(odd, sums[3:4], sums[2:3])
    bias = jnp.concatenate([q_bias, jnp.zeros((1, HW), F32), v_bias], axis=1)
    for k in range(NY):
        for j in range(SLOTS):
            hat, _ = normed(x_refs[k][j * BLK : (j + 1) * BLK, :].astype(F32))
            to = pl.multiple_of(meta[M_INV + k * SLOTS + j] * BLK, BLK)
            a1_ref[pl.ds(to, BLK), :] = (hat * gain + shift).astype(BF16)

    def project(t, carry):
        rows = pl.ds(pl.multiple_of(t * 256, 256), 256)
        joined = (dot_nn(a1_ref[rows, :], w_ref[:, 0:WQ]) + bias).astype(BF16)
        for i in range(9):
            qkv_ref[i, rows, :] = joined[:, i * HD : (i + 1) * HD]
        return carry

    lax.fori_loop(0, GROWS // 256, project, 0)

    def head(h, carry):
        for tile in TILES:
            q0, k0, count = tile
            q = qkv_ref[h, q0 : q0 + 256, :]
            k = qkv_ref[HEADS + h, k0 : k0 + count, :]
            v = qkv_ref[2 * HEADS + h, k0 : k0 + count, :]
            scores = jnp.where(visible_mask(meta, tile), dot_nt(q, k) * SCALE, MASKED_SCORE)
            top = jnp.max(scores, axis=-1, keepdims=True)
            weights = jnp.exp(scores - top)
            total = jnp.sum(weights, axis=-1, keepdims=True)
            probs = (weights * (1.0 / total)).astype(BF16)
            oh[h, q0 : q0 + 256, :] = dot_nn(probs, v)
            lse_ref[h, q0 : q0 + 256, :] = top + jnp.log(total)
        return carry

    lax.fori_loop(0, HEADS, head, 0)
    for k in range(NY):
        for j in range(SLOTS):
            rows = pl.ds(pl.multiple_of(meta[M_INV + k * SLOTS + j] * BLK, BLK), BLK)
            mixed = jnp.concatenate([oh[h, rows, :] for h in range(HEADS)], axis=1)
            o_refs[k][j * BLK : (j + 1) * BLK, :] = mixed.astype(BF16)


GELU_C = float(np.sqrt(2.0 / np.pi))


def middle_kernel(meta, *refs):
    o_refs, refs = refs[:NY], refs[NY:]
    x_ref, cot_ref, w_hbm = refs[:3]
    out_ref, dy_ref = refs[3:5]
    do_refs, refs = refs[5 : 5 + NY], refs[5 + NY :]
    g_hbm, w, g, mid, hat2, scale2, a2, a2t, dz, acc, acc_da, fcb, gvec, sems = refs
    y = meta[M_ZXY + 2]
    spans = ((0, C_FC), (C_VEC, 128), (C_FC, FF), (C_PROJ, FF))
    loads = [
        pltpu.make_async_copy(w_hbm.at[:, pl.ds(a, n)], w.at[:, pl.ds(a, n)], sems.at[i])
        for i, (a, n) in enumerate(spans)
    ]
    stores = [
        pltpu.make_async_copy(g.at[:, pl.ds(a, n)], g_hbm.at[:, pl.ds(a, n)], sems.at[4 + i])
        for i, (a, n) in enumerate(spans)
    ]
    for load in loads:
        load.start()
    offset = lax.broadcasted_iota(jnp.int32, (BLK, 1), 0)
    for j in range(SLOTS):
        rows = slice(j * BLK, (j + 1) * BLK)
        live = jnp.where(offset < meta[M_THR + j], 1.0, 0.0)
        dz[rows, :] = (cot_ref[rows, :].astype(F32) * live).astype(BF16)
    loads[0].wait()
    loads[1].wait()
    vectors = jnp.transpose(w[:, C_VEC : C_VEC + 128].astype(F32))
    out_bias, gain, shift, proj_bias = (vectors[i : i + 1] for i in range(4, 8))
    for c in range(12):
        q, s = divmod(c, 3)
        fcb[c] = jnp.broadcast_to(vectors[8 + q : 9 + q, s * 256 : (s + 1) * 256], (8, 256))
    sources = [pl.multiple_of(minus(y, k, NY) * HW, HW) for k in range(NY)]
    total = x_ref[...].astype(F32) + out_bias
    for k in range(NY):
        total = total + dot_nn(o_refs[k][...], w[pl.ds(sources[k], HW), 0:D])
    mid[...] = total
    hat, scale = normed(total)
    hat2[...] = hat
    scale2[...] = scale
    acts = hat * gain + shift
    a2[...] = acts.astype(BF16)
    a2t[...] = jnp.transpose(acts).astype(BF16)
    acc[...] = jnp.zeros_like(acc)
    acc_da[...] = jnp.zeros_like(acc_da)
    loads[2].wait()
    loads[3].wait()

    def chunk(c, carry):
        q = c // 3
        at_fc = pl.ds(pl.multiple_of(C_FC + 256 * c, 256), 256)
        at_p = pl.ds(pl.multiple_of(C_PROJ + D * q, 256), D)
        rows_p = pl.ds(pl.multiple_of(256 * (c - 3 * q), 256), 256)
        u = dot_nn(a2[...], w[:, at_fc]) + fcb[c][0:1]
        inner = GELU_C * (u + 0.044715 * (u * u * u))
        t = jnp.tanh(inner)
        m = (0.5 * u * (1.0 + t)).astype(BF16)
        slope = 0.5 * (1.0 + t) + (0.5 * GELU_C) * u * (1.0 - t * t) * (1.0 + 0.134145 * (u * u))
        p = w[rows_p, at_p]
        acc[...] += dot_nn(m, p)
        du32 = dot_nt(dz[...], p) * slope
        du = du32.astype(BF16)
        g[rows_p, at_p] = dot_tn(m, dz[...]).astype(BF16)
        g[:, at_fc] = dot_nn(a2t[...], du).astype(BF16)
        acc_da[...] += dot_nt(du, w[:, at_fc])
        fcb[c] = jnp.broadcast_to(jnp.sum(du.astype(F32), axis=0, keepdims=True), (8, 256))
        return carry

    lax.fori_loop(0, 12, chunk, 0)
    stores[2].start()
    stores[3].start()
    out_ref[...] = (mid[...] + acc[...] + proj_bias).astype(BF16)
    da2 = acc_da[...]
    gvec[...] = jnp.zeros_like(gvec)
    hat = hat2[...]
    gvec[6:7, :] = jnp.sum(da2, axis=0, keepdims=True)
    gvec[5:6, :] = jnp.sum(da2 * hat, axis=0, keepdims=True)
    dhat = da2 * gain
    mean_a = jnp.mean(dhat, axis=-1, keepdims=True)
    mean_b = jnp.mean(dhat * hat, axis=-1, keepdims=True)
    dz32 = dz[...].astype(F32)
    dy = dz32 + scale2[...] * (dhat - mean_a - hat * mean_b)
    dy_ref[...] = dy
    da = dy.astype(BF16)
    gvec[7:8, :] = jnp.sum(dz32, axis=0, keepdims=True)
    gvec[4:5, :] = jnp.sum(da.astype(F32), axis=0, keepdims=True)
    for q in range(4):
        for s in range(3):
            gvec[8 + q : 9 + q, s * 256 : (s + 1) * 256] = fcb[3 * q + s][0:1]
    for k in range(NY):
        do_refs[k][...] = dot_nt(da, w[pl.ds(sources[k], HW), 0:D]).astype(BF16)
        g[pl.ds(sources[k], HW), 0:D] = dot_tn(o_refs[k][...], da).astype(BF16)
    g[:, C_VEC : C_VEC + 128] = jnp.transpose(gvec[...]).astype(BF16)
    stores[0].start()
    stores[1].start()
    for store in stores:
        store.wait()


def back_kernel(meta, *refs):
    do_refs, refs = refs[:NY], refs[NY:]
    x_refs, refs = refs[:NY], refs[NY:]
    qkv_ref, lse_ref, a1_ref, w_ref, r0_ref, k_ref = refs[:6]
    dh_refs, refs = refs[6 : 6 + NY], refs[6 + NY :]
    gq_ref, doh, dq, dk, dv, dqkv, dh, gvec = refs
    y = meta[M_ZXY + 2]
    for k in range(NY):
        for j in range(SLOTS):
            rows = pl.ds(pl.multiple_of(meta[M_INV + k * SLOTS + j] * BLK, BLK), BLK)
            piece = do_refs[k][j * BLK : (j + 1) * BLK, :]
            for h in range(HEADS):
                doh[h, rows, :] = piece[:, h * HD : (h + 1) * HD]
    dk[...] = jnp.zeros_like(dk)
    dv[...] = jnp.zeros_like(dv)

    def head(h, carry):
        for tile in TILES:
            q0, k0, count = tile
            q = qkv_ref[h, q0 : q0 + 256, :]
            k = qkv_ref[HEADS + h, k0 : k0 + count, :]
            v = qkv_ref[2 * HEADS + h, k0 : k0 + count, :]
            do = doh[h, q0 : q0 + 256, :]
            scores = jnp.where(visible_mask(meta, tile), dot_nt(q, k) * SCALE, MASKED_SCORE)
            probs = jnp.exp(scores - lse_ref[h, q0 : q0 + 256, :])
            dp = dot_nt(do, v)
            row_dot = jnp.sum(dp * probs, axis=-1, keepdims=True)
            ds = (probs * (dp - row_dot)).astype(BF16)
            dq[h, q0 : q0 + 256, :] = dot_nn(ds, k) * SCALE
            dk[h, k0 : k0 + count, :] += dot_tn(ds, q)
            dv[h, k0 : k0 + count, :] += dot_tn(probs.astype(BF16), do)
        return carry

    lax.fori_loop(0, HEADS, head, 0)

    def join(t, carry):
        rows = pl.ds(pl.multiple_of(t * 256, 256), 256)
        parts = [dq[h, rows, :] for h in range(HEADS)]
        parts += [dk[h, rows, :] * SCALE for h in range(HEADS)]
        parts += [dv[h, rows, :] for h in range(HEADS)]
        joined = jnp.concatenate(parts, axis=1).astype(BF16)
        dqkv[rows, :] = joined
        dh[rows, :] = dot_nt(joined, w_ref[:, 0:WQ])
        return carry + jnp.sum(joined.astype(F32), axis=0, keepdims=True)

    sums = lax.fori_loop(0, GROWS // 256, join, jnp.zeros((1, WQ), F32))
    gain_sum = jnp.zeros((1, D), F32)
    shift_sum = jnp.zeros((1, D), F32)
    for k in range(NY):
        for j in range(SLOTS):
            rows = pl.ds(pl.multiple_of(meta[M_INV + k * SLOTS + j] * BLK, BLK), BLK)
            here = slice(j * BLK, (j + 1) * BLK)
            value = dh[rows, :]
            hat, _ = normed(x_refs[k][here, :].astype(F32))
            gain_sum += jnp.sum(value * hat, axis=0, keepdims=True)
            shift_sum += jnp.sum(value, axis=0, keepdims=True)
            dh_refs[k][here, :] = value.astype(dh_refs[k].dtype)
    gvec[...] = jnp.zeros_like(gvec)
    gvec[64:65, :] = gain_sum
    gvec[65:66, :] = shift_sum
    q_sum = sums[:, 0:HW]
    v_sum = sums[:, 2 * HW : 3 * HW]
    odd = k_ref[...] == 1
    for i in range(2):
        keep = odd if i else jnp.logical_not(odd)
        row = jnp.zeros((8, D), F32)
        for part, start in ((q_sum, 0), (v_sum, 384)):
            value = jnp.broadcast_to(jnp.where(keep, part, 0.0), (8, HW)).astype(BF16)
            row = row + dot_nt(value, select_matrix(r0_ref[...], start + 96 * y))
        gvec[66 + i : 67 + i, :] = row[0:1]

    def grads(c, carry):
        rows = pl.ds(pl.multiple_of(c * 256, 256), 256)
        gq_ref[rows, 0:WQ] = dot_tn(a1_ref[:, rows], dqkv[...]).astype(BF16)
        return carry

    lax.fori_loop(0, 3, grads, 0)
    gq_ref[:, WQ:QCOLS] = jnp.transpose(gvec[...])[:, 64:128].astype(BF16)


def end_kernel(*refs):
    dh_refs = refs[:NY]
    x_ref, dy_ref, gain_ref, out_ref = refs[NY:]
    dh = dh_refs[0][...]
    for k in range(1, NY):
        dh = dh + dh_refs[k][...].astype(F32)
    hat, scale = normed(x_ref[...].astype(F32))
    dhat = dh * gain_ref[0:1, :]
    mean_a = jnp.mean(dhat, axis=-1, keepdims=True)
    mean_b = jnp.mean(dhat * hat, axis=-1, keepdims=True)
    out_ref[...] = (dy_ref[...] + scale * (dhat - mean_a - hat * mean_b)).astype(BF16)


def params(mib):
    return pltpu.CompilerParams(vmem_limit_bytes=mib * 2**20)


VMEM = pl.BlockSpec(memory_space=pltpu.VMEM)
SMEM = pl.BlockSpec(memory_space=pltpu.SMEM)
ANY = pl.BlockSpec(memory_space=pl.ANY)


def cost(flops, nbytes):
    return pl.CostEstimate(flops=int(flops), bytes_accessed=int(nbytes), transcendentals=0)


def on_device(
    nz,
    nx,
    nc,
    tokens,
    slot_seq,
    slot_block_index,
    lengths,
    ln1_gain,
    ln1_bias,
    w_qkv,
    qv_bias,
    w_out,
    out_bias,
    ln2_gain,
    ln2_bias,
    w_fc,
    feed_input_bias,
    w_proj,
    proj_bias,
    cotangent,
):
    r6 = w_qkv.shape[0]
    r24 = NY * r6
    count = nz * nx * nc
    y = lax.axis_index("seq")
    f = lax.axis_index("fsdp")
    z, x, c = f // (nx * nc), (f // nc) % nx, f % nc

    def shift_y(value, k):
        return lax.ppermute(value, "seq", [(i, (i + k) % NY) for i in range(NY)])

    def shift_f(value, dz, dx, dc):
        pairs = []
        for i in range(count):
            iz, ix, ic = i // (nx * nc), (i // nc) % nx, i % nc
            to = (((iz + dz) % nz) * nx + (ix + dx) % nx) * nc + (ic + dc) % nc
            pairs.append((i, to))
        return lax.ppermute(value, "fsdp", pairs)

    def pick(value, i, axis=0):
        return lax.dynamic_index_in_dim(value, i, axis, keepdims=False)

    rel = np.arange(GSLOTS)
    absolute = ((y - rel // SLOTS) % NY) * SLOTS + rel % SLOTS
    chosen = absolute[:, None] == np.arange(GSLOTS)[None, :]
    seqs = jnp.sum(jnp.where(chosen, slot_seq[None, :], 0), axis=1)
    blocks = jnp.sum(jnp.where(chosen, slot_block_index[None, :], 0), axis=1)
    lens = jnp.sum(
        jnp.where(seqs[:, None] == np.arange(lengths.shape[1])[None, :], lengths[0:1, :], 0), axis=1
    )
    order = jnp.where(lens == LONG_LEN, 0, (seqs + 1) * 16) + blocks
    inverse = jnp.sum((order[None, :] < order[:, None]).astype(jnp.int32), axis=1)
    short = inverse[None, :] == (LONG + np.arange(4))[:, None]
    codes = jnp.sum(jnp.where(short, (seqs * SEQ_STRIDE + blocks * BLK)[None, :], 0), axis=1)
    bases = jnp.sum(jnp.where(short, (seqs * SEQ_STRIDE)[None, :], 0), axis=1)
    limits = jnp.sum(jnp.where(short, (seqs * SEQ_STRIDE + lens)[None, :], 0), axis=1)
    place = jnp.stack([z, x, y]).astype(jnp.int32)
    alive = (lens - blocks * BLK)[:SLOTS]
    meta = jnp.concatenate([inverse, codes, bases, limits, place, alive, jnp.zeros((2,), jnp.int32)])
    lane = np.arange(HW)
    r0 = jnp.asarray(((lane // (2 * r6)) * r6 + lane % r6)[None, :], jnp.int32)
    kk = jnp.asarray(((lane // r6) % 2)[None, :], jnp.int32)

    token_parts = [tokens] + [shift_y(tokens, k) for k in range(1, NY)]
    vec = jnp.concatenate(
        [
            ln1_gain[:, None],
            ln1_bias[:, None],
            qv_bias.reshape(2, r6).T,
            out_bias[:, None],
            ln2_gain[:, None],
            ln2_bias[:, None],
            proj_bias[:, None],
            feed_input_bias.reshape(r6, 4),
            jnp.zeros((r6, 116), BF16),
        ],
        axis=1,
    )
    fc_local = w_fc.reshape(r6, count, 4, r24).transpose(0, 2, 1, 3).reshape(r6, FF)
    payload = jnp.concatenate([w_qkv, w_out, fc_local, w_proj.reshape(r6, 4 * D), vec], axis=1)
    spread = lax.all_gather(payload, "seq", axis=0, tiled=False)
    v0 = 3 * D + D + 2 * FF
    vec_rows = spread[:, :, v0 : v0 + 8].reshape(r24, 8)
    qkv_mine = pick(spread[:, :, : 3 * D].reshape(r24, 3, NY, HW), y, 2).reshape(r24, WQ)
    wq_local = jnp.concatenate([qkv_mine, vec_rows, jnp.zeros((r24, 56), BF16)], axis=1)
    proj_rows = (
        spread[:, :, 4 * D + FF : v0].reshape(NY, r24, D).transpose(1, 0, 2).reshape(r24, NY * D)
    )
    fcb_rows = spread[:, :, v0 + 8 : v0 + 12].reshape(NY, r24).T
    w_local = jnp.concatenate(
        [
            spread[:, :, 3 * D : 4 * D + FF].reshape(r24, D + FF),
            proj_rows,
            vec_rows,
            fcb_rows,
            jnp.zeros((r24, 116), BF16),
        ],
        axis=1,
    )
    weights = lax.all_gather(w_local, "fsdp", axis=0, tiled=True)

    pair = wq_local
    if nc == 2:
        other = shift_f(wq_local, 0, 0, 1)
        first = jnp.where(c == 0, wq_local, other)
        second = jnp.where(c == 0, other, wq_local)
        pair = jnp.concatenate([first, second], axis=0)
    line = jnp.stack([pair] + [shift_f(pair, 0, k, 0) for k in range(1, nx)])
    planes = [line] + [shift_f(line, k, 0, 0) for k in range(1, nz)]

    front = pl.pallas_call(
        lambda *refs: front_kernel(nz, nx, *refs),
        in_specs=[SMEM] + [VMEM] * (NY + nz + 2),
        out_specs=[VMEM] * (5 + NY),
        out_shape=[
            jax.ShapeDtypeStruct((GROWS, D), BF16),
            jax.ShapeDtypeStruct((9, GROWS, HD), BF16),
            jax.ShapeDtypeStruct((HEADS, GROWS, 1), F32),
        ]
        + [jax.ShapeDtypeStruct((ROWS, HW), BF16)] * NY
        + [jax.ShapeDtypeStruct((D, QCOLS), BF16), jax.ShapeDtypeStruct((8, D), F32)],
        scratch_shapes=[pltpu.VMEM((HEADS, GROWS, HD), F32)],
        compiler_params=params(48),
        cost_estimate=cost(8e9, 15e6),
        name="front",
    )(meta, *token_parts, *planes, r0, kk)
    acts, qkv, lse = front[:3]
    mixed = front[3 : 3 + NY]
    wq, gain_one = front[3 + NY :]

    mixed_parts = [mixed[0]] + [shift_y(mixed[NY - k], k) for k in range(1, NY)]
    middle = pl.pallas_call(
        middle_kernel,
        in_specs=[SMEM] + [VMEM] * (NY + 2) + [ANY],
        out_specs=[VMEM] * (2 + NY) + [ANY],
        out_shape=[jax.ShapeDtypeStruct((ROWS, D), BF16), jax.ShapeDtypeStruct((ROWS, D), F32)]
        + [jax.ShapeDtypeStruct((ROWS, HW), BF16)] * NY
        + [jax.ShapeDtypeStruct((D, WCOLS), BF16)],
        scratch_shapes=[
            pltpu.VMEM((D, WCOLS), BF16),
            pltpu.VMEM((D, WCOLS), BF16),
            pltpu.VMEM((ROWS, D), F32),
            pltpu.VMEM((ROWS, D), F32),
            pltpu.VMEM((ROWS, 1), F32),
            pltpu.VMEM((ROWS, D), BF16),
            pltpu.VMEM((D, ROWS), BF16),
            pltpu.VMEM((ROWS, D), BF16),
            pltpu.VMEM((ROWS, D), F32),
            pltpu.VMEM((ROWS, D), F32),
            pltpu.VMEM((12, 8, 256), F32),
            pltpu.VMEM((128, D), F32),
            pltpu.SemaphoreType.DMA((8,)),
        ],
        compiler_params=params(52),
        cost_estimate=cost(13e9, 28e6),
        name="middle",
    )(meta, *mixed_parts, tokens, cotangent, weights)
    block_out, middle_grad = middle[:2]
    do_made = middle[2 : 2 + NY]
    reduced = lax.psum_scatter(middle[2 + NY], "fsdp", scatter_dimension=0, tiled=True)
    reduced = lax.optimization_barrier(reduced)

    do_parts = [do_made[0]] + [shift_y(do_made[NY - k], k) for k in range(1, NY)]
    back = pl.pallas_call(
        back_kernel,
        in_specs=[SMEM] + [VMEM] * (2 * NY + 6),
        out_specs=[VMEM] * (NY + 1),
        out_shape=[jax.ShapeDtypeStruct((ROWS, D), F32)]
        + [jax.ShapeDtypeStruct((ROWS, D), BF16)] * (NY - 1)
        + [jax.ShapeDtypeStruct((D, QCOLS), BF16)],
        scratch_shapes=[
            pltpu.VMEM((HEADS, GROWS, HD), BF16),
            pltpu.VMEM((HEADS, GROWS, HD), F32),
            pltpu.VMEM((HEADS, GROWS, HD), F32),
            pltpu.VMEM((HEADS, GROWS, HD), F32),
            pltpu.VMEM((GROWS, WQ), BF16),
            pltpu.VMEM((GROWS, D), F32),
            pltpu.VMEM((128, D), F32),
        ],
        compiler_params=params(56),
        cost_estimate=cost(12e9, 20e6),
        name="back",
    )(meta, *do_parts, *token_parts, qkv, lse, acts, wq, r0, kk)
    dh_made = back[:NY]
    dh_parts = [dh_made[0]] + [shift_y(dh_made[NY - k], k) for k in range(1, NY)]
    tokens_grad = pl.pallas_call(
        end_kernel,
        in_specs=[VMEM] * (NY + 3),
        out_specs=VMEM,
        out_shape=jax.ShapeDtypeStruct((ROWS, D), BF16),
        compiler_params=params(24),
        cost_estimate=cost(1e7, 6e6),
        name="end",
    )(*dh_parts, tokens, middle_grad, gain_one)

    def exchange(value, i, n, send):
        total = pick(value, i).astype(F32)
        for k in range(1, n):
            total = total + send(pick(value, (i + k) % n), k).astype(F32)
        return total.astype(BF16)

    gq = back[NY].reshape(nz, nx, nc, r24, QCOLS)
    if nc == 2:
        kept = pick(gq, c, 2).astype(F32)
        gq = (kept + shift_f(pick(gq, 1 - c, 2), 0, 0, 1).astype(F32)).astype(BF16)
    else:
        gq = gq[:, :, 0]
    gq = exchange(gq, z, nz, lambda v, k: shift_f(v, k, 0, 0))
    gq = exchange(gq, x, nx, lambda v, k: shift_f(v, 0, k, 0))

    row_part = jnp.concatenate(
        [reduced[:, :C_PROJ], reduced[:, C_VEC : C_VEC + 8], gq[:, WQ : WQ + 8], gq[:, :WQ]], axis=1
    ).reshape(NY, r6, C_PROJ + 16 + WQ)
    proj_part = jnp.concatenate([reduced[:, C_PROJ:C_VEC].reshape(r24, NY, D)], axis=0)
    proj_part = jnp.transpose(proj_part, (1, 0, 2))
    fcb_part = jnp.pad(reduced[:, C_VEC + 8 : C_VEC + 12].T[:, :, None], ((0, 0), (0, 0), (0, 127)))
    proj_part = jnp.concatenate([proj_part, fcb_part], axis=2)
    row_parts = [pick(row_part, y)]
    proj_parts = [pick(proj_part, y)]
    for k in range(1, NY):
        row_parts.append(shift_y(pick(row_part, (y + k) % NY), k))
        proj_parts.append(shift_y(pick(proj_part, (y + k) % NY), k))
    rows_sum = sum(part[:, : C_PROJ + 16].astype(F32) for part in row_parts)
    proj_sum = sum(part.astype(F32) for part in proj_parts)
    heads = jnp.stack([part[:, C_PROJ + 16 :] for part in row_parts])
    heads = jnp.concatenate([pick(heads, (y - q) % NY)[:, None] for q in range(NY)], axis=1)
    grad_qkv = heads.reshape(r6, NY, 3, HW).transpose(0, 2, 1, 3).reshape(r6, 3 * D).astype(F32)
    grad_fc = rows_sum[:, C_FC:C_PROJ].reshape(r6, NY, count, r24).transpose(0, 2, 1, 3)
    vecs = rows_sum[:, C_PROJ:]
    return (
        block_out,
        tokens_grad,
        vecs[:, 8],
        vecs[:, 9],
        grad_qkv,
        vecs[:, 10:12].T.reshape(2 * r6),
        rows_sum[:, :D],
        vecs[:, 4],
        vecs[:, 5],
        vecs[:, 6],
        grad_fc.reshape(r6, FF),
        proj_sum[:, D],
        proj_sum[:, :D],
        vecs[:, 7],
    )


def solution(mesh):
    both = P(("fsdp", "seq"))
    wide = P(("fsdp", "seq"), None)
    nz, nx, nc = (4, 4, 2) if mesh.shape["fsdp"] == 32 else (1, 1, mesh.shape["fsdp"])
    in_specs = (wide, P("fsdp"), P("fsdp"), P("fsdp", None), both, both, wide, both, wide)
    in_specs += (both, both, both, wide, both, wide, both, wide)
    out_specs = (wide, wide, both, both, wide, both, wide, both, both, both, wide, both, wide, both)

    def program(*args):
        return on_device(nz, nx, nc, *args)

    return jax.shard_map(
        program, mesh=mesh, in_specs=in_specs, out_specs=out_specs, check_vma=False
    )
```

time: 1360 us -> 267 us (0.20); the launches traced: 1340 us -> 266 us
  blocking collectives: 507 us -> 13.7 us
  starting transfers between devices: 262 us -> 51.8 us
  local copies, waits for them, and re-layouts: 197 us -> 30.2 us
  waiting for transfers between devices: 208 us -> 72.2 us
  matrix products: 104 us -> 0 us
  Pallas kernels: 0 us -> 79.6 us
  other arithmetic: 43.9 us -> 4.36 us
    unnamed x3 -> x0, blocking collectives: 507 us -> none
    unnamed x98 -> x1, starting transfers between devices: 262 us -> 0.04 us
    all_gather x6 -> x1, waiting for transfers between devices: 164 us -> 0.01 us  [on_device(): weights = lax.all_gather(w_local, 'fsdp', axis=0, tiled=True)]
    unnamed x294 -> x57, local copies, waits for them, and re-layouts: 147 us -> 6.2 us
    dot_general x54 -> x0, matrix products: 104 us -> none  [the longest x12 15.1 us: pair_scores(): jnp.einsum('qhd,khd->hqk', query_pair.reshape(row_count, 2, HD), key_pair...]
    pallas_call x0 -> x4, Pallas kernels: none -> 79.6 us  [the longest x1 31.1 us: on_device(): pl.pallas_call(middle_kernel, in_specs=[SMEM] + [VMEM] * (NY + 2) + [ANY]...]
    ppermute x0 -> x32, waiting for transfers between devices: none -> 52 us  [the longest x18 28.7 us: shift_y(): return lax.ppermute(value, 'seq', [(i, (i + k) % NY) for i in range(NY)])]
    ppermute x0 -> x32, starting transfers between devices: none -> 51.7 us  [the longest x18 26.7 us: shift_y(): return lax.ppermute(value, 'seq', [(i, (i + k) % NY) for i in range(NY)])]
  transfers between devices with their start and end apart: 105 -> 34, of which waited for: 10 -> 17; matrix products, arithmetic and copies ran while one was open for 46% -> 3% of each run, Pallas kernels for 0% -> 18%
where the time goes in v1:
time: 267 us; the launch traced here: 266 us
  Pallas kernels  79.6 us (30%)
  waiting for transfers between devices  72.2 us (27%)
  starting transfers between devices  51.8 us (19%)
  local copies, waits for them, and re-layouts  30.2 us (11%)
  between operations  14.6 us (5%)
  blocking collectives  13.7 us (5%)
  other arithmetic  4.36 us (2%)
    pallas_call x1, Pallas kernels, on_device(): pl.pallas_call(middle_kernel, in_specs=[SMEM] + [VMEM] * (NY + 2) + [ANY]...  31.1 us
    ppermute x18, waiting for transfers between devices, shift_y(): return lax.ppermute(value, 'seq', [(i, (i + k) % NY) for i in range(NY)])  28.7 us
    pallas_call x1, Pallas kernels, on_device(): pl.pallas_call(back_kernel, in_specs=[SMEM] + [VMEM] * (2 * NY + 6), out_...  27.1 us
    ppermute x18, starting transfers between devices, shift_y(): return lax.ppermute(value, 'seq', [(i, (i + k) % NY) for i in range(NY)])  26.7 us
    ppermute x14, starting transfers between devices, shift_f(): return lax.ppermute(value, 'fsdp', pairs)  25 us
    ppermute x14, waiting for transfers between devices, shift_f(): return lax.ppermute(value, 'fsdp', pairs)  23.2 us
    unnamed x3, waiting for transfers between devices  20.2 us
    pallas_call x1, Pallas kernels, on_device(): pl.pallas_call(lambda *refs: front_kernel(nz, nx, *refs), in_specs=[SMEM]...  18.3 us
  transfers between devices with their start and end apart: 34, of which 17 were waited for; matrix products, arithmetic and copies ran while one was open for 3% of the time, Pallas kernels for 18%

profile of v1, /device:TPU:0, one launch (start us, length us, event | category | flops | bytes accessed | tf_op | source)
XLA Modules:
  0.0 266.4 jit_solution(2686990658163841109)
XLA Ops:
  16.4 13.7 %all-gather.1 = bf16[4,6,9344]{2,1,0:T(8,128)(2,1)S(1)} all-gather(bf16[1,6,9344]{2,1,0:T(8,128)(2,1)S(1)} %bitcast.99), channel_id=2, replica_groups=mesh['fsdp'=32,'seq'=4] {'seq'}, dimensions={0}, use_global_device_ids=true | all-gather | bytes 560640 | tf_op jit(solution)/shard_map/all_gather | solution.py:441
  35.2 2.7 %collective-permute-start.5 = (bf16[48,640]{1,0:T(8,128)(2,1)S(1)}, bf16[48,640]{1,0:T(8,128)(2,1)S(1)}, u32[]{:S(2)}, u32[]{:S(2)}) collective-permute-start(bf16[48,640]{1,0:T(8,128)(2,1)S(1)} %get-tuple-element.81), channel_id=1, source_target_pairs={{0,16},{4,20},{8,24},{12,28},{16,0},{20,4},{24,8},{28,12},{32,48},... | collective-permute-start | bytes 184328 | tf_op jit(solution)/shard_map/ppermute | solution.py:398
  41.4 2.7 %collective-permute-start.1 = (bf16[384,768]{1,0:T(8,128)(2,1)S(1)}, bf16[384,768]{1,0:T(8,128)(2,1)S(1)}, u32[]{:S(2)}, u32[]{:S(2)}) collective-permute-start(bf16[384,768]{1,0:T(8,128)(2,1)S(1)} %copy-done.2), channel_id=1, source_target_pairs={{0,2},{1,3},{2,0},{3,1},{4,6},{5,7},{6,4},{7,5},{8,10},{9,11},{10,... | collective-permute-start | bytes 1769480 | tf_op jit(solution)/shard_map/ppermute | solution.py:390
  46.4 3.6 %collective-permute-start.8 = (bf16[4,48,640]{2,1,0:T(8,128)(2,1)S(1)}, bf16[4,48,640]{2,1,0:T(8,128)(2,1)S(1)}, u32[]{:S(2)}, u32[]{:S(2)}) collective-permute-start(bf16[4,48,640]{2,1,0:T(8,128)(2,1)S(1)} %pad_maximum_fusion.refs_5_), channel_id=1, source_target_pairs={{0,64},{4,68},{8,72},{12,76},{16,80},{20,84},{24,88},{28,92},{32,9... | collective-permute-start | bytes 737288 | tf_op jit(solution)/shard_map/ppermute | solution.py:398
  50.0 8.3 %collective-permute-done.7.refs_6_ = bf16[4,48,640]{2,1,0:T(8,128)(2,1)S(1)} collective-permute-done((bf16[4,48,640]{2,1,0:T(8,128)(2,1)S(1)}, bf16[4,48,640]{2,1,0:T(8,128)(2,1)S(1)}, u32[]{:S(2)}, u32[]{:S(2)}) %collective-permute-start.7) | collective-permute-done | bytes 245792 | tf_op jit(solution)/shard_map/ppermute | solution.py:398
  61.0 3.6 %collective-permute-done.8.refs_7_ = bf16[4,48,640]{2,1,0:T(8,128)(2,1)S(1)} collective-permute-done((bf16[4,48,640]{2,1,0:T(8,128)(2,1)S(1)}, bf16[4,48,640]{2,1,0:T(8,128)(2,1)S(1)}, u32[]{:S(2)}, u32[]{:S(2)}) %collective-permute-start.8) | collective-permute-done | bytes 245792 | tf_op jit(solution)/shard_map/ppermute | solution.py:398
  64.6 4.6 %collective-permute-done.1.refs_3_.refs_6_ = bf16[384,768]{1,0:T(8,128)(2,1)S(1)} collective-permute-done((bf16[384,768]{1,0:T(8,128)(2,1)S(1)}, bf16[384,768]{1,0:T(8,128)(2,1)S(1)}, u32[]{:S(2)}, u32[]{:S(2)}) %collective-permute-start.1) | collective-permute-done | bytes 589856 | tf_op jit(solution)/shard_map/ppermute | solution.py:390
  69.3 18.3 %front.1 = (bf16[1536,768]{1,0:T(8,128)(2,1)}, bf16[9,1536,64]{2,1,0:T(8,128)(2,1)}, f32[3,1536,1]{2,1,0:T(8,128)}, bf16[384,192]{1,0:T(8,128)(2,1)S(1)}, bf16[3...) custom-call(s32[32]{0:T(128)S(1)} %concatenate.33.refs_0_.meta, ...), custom_call_target="tpu_custom_call" | custom-call | flops 8000000000 | bytes 15000000 | tf_op jit(solution)/shard_map/front/pallas_call | solution.py:471
  90.7 2.7 %collective-permute-start.11 = (bf16[384,192]{1,0:T(8,128)(2,1)S(1)}, bf16[384,192]{1,0:T(8,128)(2,1)S(1)}, u32[]{:S(2)}, u32[]{:S(2)}) collective-permute-start(bf16[384,192]{1,0:T(8,128)(2,1)S(1)} %get-tuple-element.37), channel_id=1, source_target_pairs={{0,2},{1,3},{2,0},{3,1},{4,6},{5,7},{6,4},{7,5},{8,10},{9,11},{10,... | collective-permute-start | bytes 442376 | tf_op jit(solution)/shard_map/ppermute | solution.py:390
  94.0 3.0 %collective-permute-done.10.refs_1_ = bf16[384,192]{1,0:T(8,128)(2,1)S(1)} collective-permute-done((bf16[384,192]{1,0:T(8,128)(2,1)S(1)}, bf16[384,192]{1,0:T(8,128)(2,1)S(1)}, u32[]{:S(2)}, u32[]{:S(2)}) %collective-permute-start.10) | collective-permute-done | bytes 147488 | tf_op jit(solution)/shard_map/ppermute | solution.py:390
  96.9 5.4 %collective-permute-done.11.refs_2_ = bf16[384,192]{1,0:T(8,128)(2,1)S(1)} collective-permute-done((bf16[384,192]{1,0:T(8,128)(2,1)S(1)}, bf16[384,192]{1,0:T(8,128)(2,1)S(1)}, u32[]{:S(2)}, u32[]{:S(2)}) %collective-permute-start.11) | collective-permute-done | bytes 147488 | tf_op jit(solution)/shard_map/ppermute | solution.py:390
  103.3 31.1 %middle.1 = (bf16[384,768]{1,0:T(8,128)(2,1)}, f32[384,768]{1,0:T(8,128)}, bf16[384,192]{1,0:T(8,128)(2,1)S(1)}, bf16[384,192]{1,0:T(8,128)(2,1)S(1)}, bf16[384,...) custom-call(s32[32]{0:T(128)S(1)} %concatenate.33.refs_0_.meta, ...), custom_call_target="tpu_custom_call" | custom-call | flops 12999999488 | bytes 28000000 | tf_op jit(solution)/shard_map/middle/pallas_call | solution.py:492
  136.0 2.6 collective-permute-start.14
  139.3 3.5 %collective-permute-done.13.refs_1_ = bf16[384,192]{1,0:T(8,128)(2,1)S(1)} collective-permute-done((bf16[384,192]{1,0:T(8,128)(2,1)S(1)}, bf16[384,192]{1,0:T(8,128)(2,1)S(1)}, u32[]{:S(2)}, u32[]{:S(2)}) %collective-permute-start.13) | collective-permute-done | bytes 147488 | tf_op jit(solution)/shard_map/ppermute | solution.py:390
  142.8 4.5 %collective-permute-done.14.refs_2_ = bf16[384,192]{1,0:T(8,128)(2,1)S(1)} collective-permute-done((bf16[384,192]{1,0:T(8,128)(2,1)S(1)}, bf16[384,192]{1,0:T(8,128)(2,1)S(1)}, u32[]{:S(2)}, u32[]{:S(2)}) %collective-permute-start.14) | collective-permute-done | bytes 147488 | tf_op jit(solution)/shard_map/ppermute | solution.py:390
  148.1 27.1 %back.1 = (f32[384,768]{1,0:T(8,128)}, bf16[384,768]{1,0:T(8,128)(2,1)}, bf16[384,768]{1,0:T(8,128)(2,1)}, bf16[384,768]{1,0:T(8,128)(2,1)}, bf16[768,640]{1,0:T(8,128)(2,1)}) custom-call(s32[32]{0:T(128)} %copy-done.6, bf16[384,192]{1,0:T(8,128)(2,1)} %copy-done.15, bf16[384,192]{1,0:T(8,128)(2,1)} %copy-done.24, bf16[384,192]{1,0:T(8,128)(2,1)} %copy-done.25, ...), custom_call_target="tpu_custom_call" | custom-call | flops 12000000000 | bytes 20000000 | tf_op jit(solution)/shard_map/back/pallas_call | solution.py:524
  183.8 2.7 %collective-permute-start.17 = (bf16[384,768]{1,0:T(8,128)(2,1)}, bf16[384,768]{1,0:T(8,128)(2,1)}, u32[]{:S(2)}, u32[]{:S(2)}) collective-permute-start(bf16[384,768]{1,0:T(8,128)(2,1)} %get-tuple-element.50), channel_id=1, source_target_pairs={{0,2},{1,3},{2,0},{3,1},{4,6},{5,7},{6,4},{7,5},{8,10},{9,11},{10,... | collective-permute-start | bytes 1769480 | tf_op jit(solution)/shard_map/ppermute | solution.py:390
  187.2 3.5 %collective-permute-start.21 = (bf16[4,24,640]{2,1,0:T(8,128)(2,1)}, bf16[4,24,640]{2,1,0:T(8,128)(2,1)}, u32[]{:S(2)}, u32[]{:S(2)}) collective-permute-start(bf16[4,24,640]{2,1,0:T(8,128)(2,1)} %get-tuple-element.69), channel_id=1, source_target_pairs={{0,64},{4,68},{8,72},{12,76},{16,80},{20,84},{24,88},{28,92},{32,9... | collective-permute-start | bytes 368648 | tf_op jit(solution)/shard_map/ppermute | solution.py:398
  193.7 4.0 %collective-permute-done.21 = bf16[4,24,640]{2,1,0:T(8,128)(2,1)} collective-permute-done((bf16[4,24,640]{2,1,0:T(8,128)(2,1)}, bf16[4,24,640]{2,1,0:T(8,128)(2,1)}, u32[]{:S(2)}, u32[]{:S(2)}) %collective-permute-start.21) | collective-permute-done | bytes 122912 | tf_op jit(solution)/shard_map/ppermute | solution.py:398
  197.7 4.3 %collective-permute-done.22 = bf16[4,24,640]{2,1,0:T(8,128)(2,1)} collective-permute-done((bf16[4,24,640]{2,1,0:T(8,128)(2,1)}, bf16[4,24,640]{2,1,0:T(8,128)(2,1)}, u32[]{:S(2)}, u32[]{:S(2)}) %collective-permute-start.22) | collective-permute-done | bytes 122912 | tf_op jit(solution)/shard_map/ppermute | solution.py:398
  207.4 5.2 %collective-permute-done.17.refs_2_ = bf16[384,768]{1,0:T(8,128)(2,1)} collective-permute-done((bf16[384,768]{1,0:T(8,128)(2,1)}, bf16[384,768]{1,0:T(8,128)(2,1)}, u32[]{:S(2)}, u32[]{:S(2)}) %collective-permute-start.17) | collective-permute-done | bytes 589856 | tf_op jit(solution)/shard_map/ppermute | solution.py:390
  213.4 3.0 %end.1 = bf16[384,768]{1,0:T(8,128)(2,1)} custom-call(f32[384,768]{1,0:T(8,128)S(1)} %copy-done.1, bf16[384,768]{1,0:T(8,128)(2,1)S(1)} %collective-permute-done.16.refs_1_, bf16[384,768]{1,0:T(8,128)(2,1)} %collective-permute-done.17.refs_2_, bf16[384,768]{1,0:T(8,128)(2,1)} %collective-permute-done.18.refs_3_, bf16[384,768]{1,0:T(8,128)(2,1)S(1)} %copy-done.3, ...), custom_call_target="tpu_custom_call" | custom-call | flops 10000000 | bytes 6000000 | tf_op jit(solution)/shard_map/end/pallas_call | solution.py:546
  217.3 20.2 %reduce-scatter.4.cloned.1.call-done = bf16[24,7040]{1,0:T(8,128)(2,1)} async-done(((bf16[768,7040]{1,0:T(8,128)(2,1)}), bf16[24,7040]{1,0:T(8,128)(2,1)}) %reduce-scatter.4.cloned.1.call-update) | async-done | bytes 337936
  242.6 2.7 %collective-permute-start.30 = (bf16[24,896]{1,0:T(8,128)(2,1)S(1)}, bf16[24,896]{1,0:T(8,128)(2,1)S(1)}, u32[]{:S(2)}, u32[]{:S(2)}) collective-permute-start(bf16[24,896]{1,0:T(8,128)(2,1)S(1)} %get-tuple-element.76), channel_id=1, source_target_pairs={{0,2},{1,3},{2,0},{3,1},{4,6},{5,7},{6,4},{7,5},{8,10},{9,11},{10,... | collective-permute-start | bytes 129032 | tf_op jit(solution)/shard_map/ppermute | solution.py:390
  (196 shorter events, 68.7 us)
Async XLA Ops:
  7.2 95.2 %all-gather.4.cloned.1.call-start = ((), (), s32[]{:S(2)}) async-start(), calls=%async_computation.1 | async-start | bytes 11151360 | tf_op jit(solution)/shard_map/all_gather | solution.py:460
  31.5 206.0 %reduce-scatter.4.cloned.1.call-start = ((), (), s32[]{:S(2)}) async-start(), calls=%async_computation.2 | async-start | bytes 11151360
  33.6 10.5 %collective-permute-start.4 = (bf16[48,640]{1,0:T(8,128)(2,1)S(1)}, bf16[48,640]{1,0:T(8,128)(2,1)S(1)}, u32[]{:S(2)}, u32[]{:S(2)}) collective-permute-start(bf16[48,640]{1,0:T(8,128)(2,1)S(1)} %get-tuple-element.81), channel_id=1, source_target_pairs={{0,8},{4,12},{8,16},{12,20},{16,24},{20,28},{24,0},{28,4},{32,40},... | collective-permute-start | bytes 184328 | tf_op jit(solution)/shard_map/ppermute | solution.py:398
  35.2 8.9 %collective-permute-start.5 = (bf16[48,640]{1,0:T(8,128)(2,1)S(1)}, bf16[48,640]{1,0:T(8,128)(2,1)S(1)}, u32[]{:S(2)}, u32[]{:S(2)}) collective-permute-start(bf16[48,640]{1,0:T(8,128)(2,1)S(1)} %get-tuple-element.81), channel_id=1, source_target_pairs={{0,16},{4,20},{8,24},{12,28},{16,0},{20,4},{24,8},{28,12},{32,48},... | collective-permute-start | bytes 184328 | tf_op jit(solution)/shard_map/ppermute | solution.py:398
  39.3 25.3 %collective-permute-start = (bf16[384,768]{1,0:T(8,128)(2,1)S(1)}, bf16[384,768]{1,0:T(8,128)(2,1)S(1)}, u32[]{:S(2)}, u32[]{:S(2)}) collective-permute-start(bf16[384,768]{1,0:T(8,128)(2,1)S(1)} %copy-done.2), channel_id=1, source_target_pairs={{0,1},{1,2},{2,3},{3,0},{4,5},{5,6},{6,7},{7,4},{8,9},{9,10},{10,1... | collective-permute-start | bytes 1769480 | tf_op jit(solution)/shard_map/ppermute | solution.py:390
  41.4 27.8 %collective-permute-start.1 = (bf16[384,768]{1,0:T(8,128)(2,1)S(1)}, bf16[384,768]{1,0:T(8,128)(2,1)S(1)}, u32[]{:S(2)}, u32[]{:S(2)}) collective-permute-start(bf16[384,768]{1,0:T(8,128)(2,1)S(1)} %copy-done.2), channel_id=1, source_target_pairs={{0,2},{1,3},{2,0},{3,1},{4,6},{5,7},{6,4},{7,5},{8,10},{9,11},{10,... | collective-permute-start | bytes 1769480 | tf_op jit(solution)/shard_map/ppermute | solution.py:390
  44.1 25.2 %collective-permute-start.2 = (bf16[384,768]{1,0:T(8,128)(2,1)S(1)}, bf16[384,768]{1,0:T(8,128)(2,1)S(1)}, u32[]{:S(2)}, u32[]{:S(2)}) collective-permute-start(bf16[384,768]{1,0:T(8,128)(2,1)S(1)} %copy-done.2), channel_id=1, source_target_pairs={{0,3},{1,0},{2,1},{3,2},{4,7},{5,4},{6,5},{7,6},{8,11},{9,8},{10,9... | collective-permute-start | bytes 1769480 | tf_op jit(solution)/shard_map/ppermute | solution.py:390
  44.1 14.2 %collective-permute-start.7 = (bf16[4,48,640]{2,1,0:T(8,128)(2,1)S(1)}, bf16[4,48,640]{2,1,0:T(8,128)(2,1)S(1)}, u32[]{:S(2)}, u32[]{:S(2)}) collective-permute-start(bf16[4,48,640]{2,1,0:T(8,128)(2,1)S(1)} %pad_maximum_fusion.refs_5_), channel_id=1, source_target_pairs={{0,32},{4,36},{8,40},{12,44},{16,48},{20,52},{24,56},{28,60},{32,6... | collective-permute-start | bytes 737288 | tf_op jit(solution)/shard_map/ppermute | solution.py:398
  46.4 18.2 %collective-permute-start.8 = (bf16[4,48,640]{2,1,0:T(8,128)(2,1)S(1)}, bf16[4,48,640]{2,1,0:T(8,128)(2,1)S(1)}, u32[]{:S(2)}, u32[]{:S(2)}) collective-permute-start(bf16[4,48,640]{2,1,0:T(8,128)(2,1)S(1)} %pad_maximum_fusion.refs_5_), channel_id=1, source_target_pairs={{0,64},{4,68},{8,72},{12,76},{16,80},{20,84},{24,88},{28,92},{32,9... | collective-permute-start | bytes 737288 | tf_op jit(solution)/shard_map/ppermute | solution.py:398
  90.7 11.7 %collective-permute-start.11 = (bf16[384,192]{1,0:T(8,128)(2,1)S(1)}, bf16[384,192]{1,0:T(8,128)(2,1)S(1)}, u32[]{:S(2)}, u32[]{:S(2)}) collective-permute-start(bf16[384,192]{1,0:T(8,128)(2,1)S(1)} %get-tuple-element.37), channel_id=1, source_target_pairs={{0,2},{1,3},{2,0},{3,1},{4,6},{5,7},{6,4},{7,5},{8,10},{9,11},{10,... | collective-permute-start | bytes 442376 | tf_op jit(solution)/shard_map/ppermute | solution.py:390
  93.3 9.0 %collective-permute-start.12 = (bf16[384,192]{1,0:T(8,128)(2,1)S(1)}, bf16[384,192]{1,0:T(8,128)(2,1)S(1)}, u32[]{:S(2)}, u32[]{:S(2)}) collective-permute-start(bf16[384,192]{1,0:T(8,128)(2,1)S(1)} %get-tuple-element.38), channel_id=1, source_target_pairs={{0,3},{1,0},{2,1},{3,2},{4,7},{5,4},{6,5},{7,6},{8,11},{9,8},{10,9... | collective-permute-start | bytes 442376 | tf_op jit(solution)/shard_map/ppermute | solution.py:390
  135.1 7.8 %collective-permute-start.13 = (bf16[384,192]{1,0:T(8,128)(2,1)S(1)}, bf16[384,192]{1,0:T(8,128)(2,1)S(1)}, u32[]{:S(2)}, u32[]{:S(2)}) collective-permute-start(bf16[384,192]{1,0:T(8,128)(2,1)S(1)} %get-tuple-element.41), channel_id=1, source_target_pairs={{0,1},{1,2},{2,3},{3,0},{4,5},{5,6},{6,7},{7,4},{8,9},{9,10},{10,1... | collective-permute-start | bytes 442376 | tf_op jit(solution)/shard_map/ppermute | solution.py:390
  136.0 11.3 %collective-permute-start.14 = (bf16[384,192]{1,0:T(8,128)(2,1)S(1)}, bf16[384,192]{1,0:T(8,128)(2,1)S(1)}, u32[]{:S(2)}, u32[]{:S(2)}) collective-permute-start(bf16[384,192]{1,0:T(8,128)(2,1)S(1)} %get-tuple-element.42), channel_id=1, source_target_pairs={{0,2},{1,3},{2,0},{3,1},{4,6},{5,7},{6,4},{7,5},{8,10},{9,11},{10,... | collective-permute-start | bytes 442376 | tf_op jit(solution)/shard_map/ppermute | solution.py:390
  138.7 8.7 %collective-permute-start.15 = (bf16[384,192]{1,0:T(8,128)(2,1)S(1)}, bf16[384,192]{1,0:T(8,128)(2,1)S(1)}, u32[]{:S(2)}, u32[]{:S(2)}) collective-permute-start(bf16[384,192]{1,0:T(8,128)(2,1)S(1)} %get-tuple-element.43), channel_id=1, source_target_pairs={{0,3},{1,0},{2,1},{3,2},{4,7},{5,4},{6,5},{7,6},{8,11},{9,8},{10,9... | collective-permute-start | bytes 442376 | tf_op jit(solution)/shard_map/ppermute | solution.py:390
  180.7 10.1 %collective-permute-start.20 = (bf16[4,24,640]{2,1,0:T(8,128)(2,1)S(1)}, bf16[4,24,640]{2,1,0:T(8,128)(2,1)S(1)}, u32[]{:S(2)}, u32[]{:S(2)}) collective-permute-start(bf16[4,24,640]{2,1,0:T(8,128)(2,1)S(1)} %get-tuple-element.67), channel_id=1, source_target_pairs={{0,32},{4,36},{8,40},{12,44},{16,48},{20,52},{24,56},{28,60},{32,6... | collective-permute-start | bytes 368648 | tf_op jit(solution)/shard_map/ppermute | solution.py:398
  182.7 23.0 %collective-permute-start.16 = (bf16[384,768]{1,0:T(8,128)(2,1)}, bf16[384,768]{1,0:T(8,128)(2,1)S(1)}, u32[]{:S(2)}, u32[]{:S(2)}) collective-permute-start(bf16[384,768]{1,0:T(8,128)(2,1)} %get-tuple-element.49), channel_id=1, source_target_pairs={{0,1},{1,2},{2,3},{3,0},{4,5},{5,6},{6,7},{7,4},{8,9},{9,10},{10,1... | collective-permute-start | bytes 1769480 | tf_op jit(solution)/shard_map/ppermute | solution.py:390
  183.8 28.7 %collective-permute-start.17 = (bf16[384,768]{1,0:T(8,128)(2,1)}, bf16[384,768]{1,0:T(8,128)(2,1)}, u32[]{:S(2)}, u32[]{:S(2)}) collective-permute-start(bf16[384,768]{1,0:T(8,128)(2,1)} %get-tuple-element.50), channel_id=1, source_target_pairs={{0,2},{1,3},{2,0},{3,1},{4,6},{5,7},{6,4},{7,5},{8,10},{9,11},{10,... | collective-permute-start | bytes 1769480 | tf_op jit(solution)/shard_map/ppermute | solution.py:390
  186.5 26.1 %collective-permute-start.18 = (bf16[384,768]{1,0:T(8,128)(2,1)}, bf16[384,768]{1,0:T(8,128)(2,1)}, u32[]{:S(2)}, u32[]{:S(2)}) collective-permute-start(bf16[384,768]{1,0:T(8,128)(2,1)} %get-tuple-element.51), channel_id=1, source_target_pairs={{0,3},{1,0},{2,1},{3,2},{4,7},{5,4},{6,5},{7,6},{8,11},{9,8},{10,9... | collective-permute-start | bytes 1769480 | tf_op jit(solution)/shard_map/ppermute | solution.py:390
  187.2 10.5 %collective-permute-start.21 = (bf16[4,24,640]{2,1,0:T(8,128)(2,1)}, bf16[4,24,640]{2,1,0:T(8,128)(2,1)}, u32[]{:S(2)}, u32[]{:S(2)}) collective-permute-start(bf16[4,24,640]{2,1,0:T(8,128)(2,1)} %get-tuple-element.69), channel_id=1, source_target_pairs={{0,64},{4,68},{8,72},{12,76},{16,80},{20,84},{24,88},{28,92},{32,9... | collective-permute-start | bytes 368648 | tf_op jit(solution)/shard_map/ppermute | solution.py:398
  191.4 10.6 %collective-permute-start.22 = (bf16[4,24,640]{2,1,0:T(8,128)(2,1)}, bf16[4,24,640]{2,1,0:T(8,128)(2,1)}, u32[]{:S(2)}, u32[]{:S(2)}) collective-permute-start(bf16[4,24,640]{2,1,0:T(8,128)(2,1)} %get-tuple-element.68), channel_id=1, source_target_pairs={{0,96},{4,100},{8,104},{12,108},{16,112},{20,116},{24,120},{28,124... | collective-permute-start | bytes 368648 | tf_op jit(solution)/shard_map/ppermute | solution.py:398
  203.8 12.6 %collective-permute-start.23 = (bf16[24,640]{1,0:T(8,128)(2,1)}, bf16[24,640]{1,0:T(8,128)(2,1)}, u32[]{:S(2)}, u32[]{:S(2)}) collective-permute-start(bf16[24,640]{1,0:T(8,128)(2,1)} %get-tuple-element.77), channel_id=1, source_target_pairs={{0,8},{4,12},{8,16},{12,20},{16,24},{20,28},{24,0},{28,4},{32,40},... | collective-permute-start | bytes 92168 | tf_op jit(solution)/shard_map/ppermute | solution.py:398
  204.4 12.0 %collective-permute-start.24 = (bf16[24,640]{1,0:T(8,128)(2,1)}, bf16[24,640]{1,0:T(8,128)(2,1)}, u32[]{:S(2)}, u32[]{:S(2)}) collective-permute-start(bf16[24,640]{1,0:T(8,128)(2,1)} %get-tuple-element.79), channel_id=1, source_target_pairs={{0,16},{4,20},{8,24},{12,28},{16,0},{20,4},{24,8},{28,12},{32,48},... | collective-permute-start | bytes 92168 | tf_op jit(solution)/shard_map/ppermute | solution.py:398
  205.7 10.7 %collective-permute-start.25 = (bf16[24,640]{1,0:T(8,128)(2,1)}, bf16[24,640]{1,0:T(8,128)(2,1)}, u32[]{:S(2)}, u32[]{:S(2)}) collective-permute-start(bf16[24,640]{1,0:T(8,128)(2,1)} %get-tuple-element.78), channel_id=1, source_target_pairs={{0,24},{4,28},{8,0},{12,4},{16,8},{20,12},{24,16},{28,20},{32,56},... | collective-permute-start | bytes 92168 | tf_op jit(solution)/shard_map/ppermute | solution.py:398
  242.6 8.0 %collective-permute-start.30 = (bf16[24,896]{1,0:T(8,128)(2,1)S(1)}, bf16[24,896]{1,0:T(8,128)(2,1)S(1)}, u32[]{:S(2)}, u32[]{:S(2)}) collective-permute-start(bf16[24,896]{1,0:T(8,128)(2,1)S(1)} %get-tuple-element.76), channel_id=1, source_target_pairs={{0,2},{1,3},{2,0},{3,1},{4,6},{5,7},{6,4},{7,5},{8,10},{9,11},{10,... | collective-permute-start | bytes 129032 | tf_op jit(solution)/shard_map/ppermute | solution.py:390
  (38 other events, 494.4 us)
Sparse Core Ops, SparseCore 0:
  31.6 65.3 all-gather.3
  135.2 102.2 reduce-scatter.3

commit v2 on v1

--- a/solution.py
+++ b/solution.py
@@ -30,7 +30,7 @@
 MASKED_SCORE = -1e30
 SCALE = HD**-0.5
 SEQ_STRIDE = 4096
-M_INV, M_CODE, M_BASE, M_LIM, M_ZXY, M_THR = 0, 12, 16, 20, 24, 27
+M_INV, M_CODE, M_BASE, M_LIM, M_ZXY, M_THR, M_CORE = 0, 12, 16, 20, 24, 27, 30
 F32 = jnp.float32
 BF16 = jnp.bfloat16
 TILES = tuple((256 * t, 0, 256 * (t + 1)) for t in range(4)) + ((1024, 1024, 256), (1280, 1024, 512))
@@ -154,21 +154,40 @@
 GELU_C = float(np.sqrt(2.0 / np.pi))
 
 
+def hidden_step(q, w, bias, a2, a2t, dz, acc, acc_da, g):
+    at_fc = slice(q * D, (q + 1) * D)
+    at_p = slice((4 + q) * D, (5 + q) * D)
+    u = dot_nn(a2[...], w[:, at_fc]) + bias
+    t = jnp.tanh(GELU_C * (u + 0.044715 * (u * u * u)))
+    m = (0.5 * u * (1.0 + t)).astype(BF16)
+    slope = 0.5 * (1.0 + t) + (0.5 * GELU_C) * u * (1.0 - t * t) * (1.0 + 0.134145 * (u * u))
+    du = (dot_nt(dz[...], w[:, at_p]) * slope).astype(BF16)
+    g[:, at_p] = dot_tn(m, dz[...]).astype(BF16)
+    g[:, at_fc] = dot_nn(a2t[...], du).astype(BF16)
+    acc[...] += dot_nn(m, w[:, at_p])
+    acc_da[...] += dot_nt(du, w[:, at_fc])
+    return jnp.sum(du.astype(F32), axis=0, keepdims=True)
+
+
 def middle_kernel(meta, *refs):
     o_refs, refs = refs[:NY], refs[NY:]
     x_ref, cot_ref, w_hbm = refs[:3]
     out_ref, dy_ref = refs[3:5]
     do_refs, refs = refs[5 : 5 + NY], refs[5 + NY :]
-    g_hbm, w, g, mid, hat2, scale2, a2, a2t, dz, acc, acc_da, fcb, gvec, sems = refs
+    rest, g_hbm, w, g, gw, hat2, dz, a2, a2t, acc, acc_da, gvec, sems = refs
     y = meta[M_ZXY + 2]
-    spans = ((0, C_FC), (C_VEC, 128), (C_FC, FF), (C_PROJ, FF))
+    spans = [(0, 8 * D, D), (C_VEC, 9 * D, 128)]
+    for q in range(4):
+        spans += [(C_FC + q * D, q * D, D), (C_PROJ + q * D, (4 + q) * D, D)]
     loads = [
-        pltpu.make_async_copy(w_hbm.at[:, pl.ds(a, n)], w.at[:, pl.ds(a, n)], sems.at[i])
-        for i, (a, n) in enumerate(spans)
+        pltpu.make_async_copy(w_hbm.at[:, pl.ds(a, n)], w.at[:, pl.ds(b, n)], sems.at[i])
+        for i, (a, b, n) in enumerate(spans)
     ]
     stores = [
-        pltpu.make_async_copy(g.at[:, pl.ds(a, n)], g_hbm.at[:, pl.ds(a, n)], sems.at[4 + i])
-        for i, (a, n) in enumerate(spans)
+        pltpu.make_async_copy(
+            g.at[:, pl.ds(i * D, D)], g_hbm.at[:, pl.ds(i * D, D)], sems.at[10 + i]
+        )
+        for i in range(8)
     ]
     for load in loads:
         load.start()
@@ -179,84 +198,174 @@
         dz[rows, :] = (cot_ref[rows, :].astype(F32) * live).astype(BF16)
     loads[0].wait()
     loads[1].wait()
-    vectors = jnp.transpose(w[:, C_VEC : C_VEC + 128].astype(F32))
-    out_bias, gain, shift, proj_bias = (vectors[i : i + 1] for i in range(4, 8))
-    for c in range(12):
-        q, s = divmod(c, 3)
-        fcb[c] = jnp.broadcast_to(vectors[8 + q : 9 + q, s * 256 : (s + 1) * 256], (8, 256))
-    sources = [pl.multiple_of(minus(y, k, NY) * HW, HW) for k in range(NY)]
-    total = x_ref[...].astype(F32) + out_bias
+    vec = jnp.transpose(w[:, 9 * D : 9 * D + 128].astype(F32))
+    total = x_ref[...].astype(F32) + vec[4:5, :]
     for k in range(NY):
-        total = total + dot_nn(o_refs[k][...], w[pl.ds(sources[k], HW), 0:D])
-    mid[...] = total
+        at = pl.ds(pl.multiple_of(minus(y, k, NY) * HW, HW), HW)
+        total = total + dot_nn(o_refs[k][...], w[at, 8 * D : 9 * D])
     hat, scale = normed(total)
     hat2[...] = hat
-    scale2[...] = scale
-    acts = hat * gain + shift
+    acts = hat * vec[5:6, :] + vec[6:7, :]
     a2[...] = acts.astype(BF16)
     a2t[...] = jnp.transpose(acts).astype(BF16)
-    acc[...] = jnp.zeros_like(acc)
+    acc[...] = total + vec[7:8, :]
     acc_da[...] = jnp.zeros_like(acc_da)
-    loads[2].wait()
-    loads[3].wait()
-
-    def chunk(c, carry):
-        q = c // 3
-        at_fc = pl.ds(pl.multiple_of(C_FC + 256 * c, 256), 256)
-        at_p = pl.ds(pl.multiple_of(C_PROJ + D * q, 256), D)
-        rows_p = pl.ds(pl.multiple_of(256 * (c - 3 * q), 256), 256)
-        u = dot_nn(a2[...], w[:, at_fc]) + fcb[c][0:1]
-        inner = GELU_C * (u + 0.044715 * (u * u * u))
-        t = jnp.tanh(inner)
-        m = (0.5 * u * (1.0 + t)).astype(BF16)
-        slope = 0.5 * (1.0 + t) + (0.5 * GELU_C) * u * (1.0 - t * t) * (1.0 + 0.134145 * (u * u))
-        p = w[rows_p, at_p]
-        acc[...] += dot_nn(m, p)
-        du32 = dot_nt(dz[...], p) * slope
-        du = du32.astype(BF16)
-        g[rows_p, at_p] = dot_tn(m, dz[...]).astype(BF16)
-        g[:, at_fc] = dot_nn(a2t[...], du).astype(BF16)
-        acc_da[...] += dot_nt(du, w[:, at_fc])
-        fcb[c] = jnp.broadcast_to(jnp.sum(du.astype(F32), axis=0, keepdims=True), (8, 256))
-        return carry
-
-    lax.fori_loop(0, 12, chunk, 0)
-    stores[2].start()
-    stores[3].start()
-    out_ref[...] = (mid[...] + acc[...] + proj_bias).astype(BF16)
+    gvec[...] = jnp.zeros_like(gvec)
+    for q in range(4):
+        loads[2 + 2 * q].wait()
+        loads[3 + 2 * q].wait()
+        row = hidden_step(q, w, vec[8 + q : 9 + q, :], a2, a2t, dz, acc, acc_da, g)
+        gvec[8 + q : 9 + q, :] = row
+        stores[q].start()
+        stores[4 + q].start()
+    out_ref[...] = acc[...].astype(BF16)
     da2 = acc_da[...]
-    gvec[...] = jnp.zeros_like(gvec)
     hat = hat2[...]
     gvec[6:7, :] = jnp.sum(da2, axis=0, keepdims=True)
     gvec[5:6, :] = jnp.sum(da2 * hat, axis=0, keepdims=True)
-    dhat = da2 * gain
+    dhat = da2 * vec[5:6, :]
     mean_a = jnp.mean(dhat, axis=-1, keepdims=True)
     mean_b = jnp.mean(dhat * hat, axis=-1, keepdims=True)
     dz32 = dz[...].astype(F32)
-    dy = dz32 + scale2[...] * (dhat - mean_a - hat * mean_b)
+    dy = dz32 + scale * (dhat - mean_a - hat * mean_b)
     dy_ref[...] = dy
     da = dy.astype(BF16)
     gvec[7:8, :] = jnp.sum(dz32, axis=0, keepdims=True)
     gvec[4:5, :] = jnp.sum(da.astype(F32), axis=0, keepdims=True)
-    for q in range(4):
-        for s in range(3):
-            gvec[8 + q : 9 + q, s * 256 : (s + 1) * 256] = fcb[3 * q + s][0:1]
     for k in range(NY):
-        do_refs[k][...] = dot_nt(da, w[pl.ds(sources[k], HW), 0:D]).astype(BF16)
-        g[pl.ds(sources[k], HW), 0:D] = dot_tn(o_refs[k][...], da).astype(BF16)
-    g[:, C_VEC : C_VEC + 128] = jnp.transpose(gvec[...]).astype(BF16)
-    stores[0].start()
-    stores[1].start()
+        at = pl.ds(pl.multiple_of(minus(y, k, NY) * HW, HW), HW)
+        do_refs[k][...] = dot_nt(da, w[at, 8 * D : 9 * D]).astype(BF16)
+        gw[at, :] = dot_tn(o_refs[k][...], da)
+    rest[:, 0:D] = gw[...].astype(BF16)
+    rest[:, D : D + 128] = jnp.transpose(gvec[...]).astype(BF16)
     for store in stores:
         store.wait()
 
 
-def back_kernel(meta, *refs):
+def hidden_order(count, r24):
+    return [
+        (d * 4 * r24 + q * r24, (q * count + d) * r24) for q in range(NY) for d in range(count)
+    ]
+
+
+def pack_kernel(count, r6, *refs):
+    sources, out, wide, vec = refs[:12], refs[12], refs[13], refs[14]
+    local, sems = refs[15:27], refs[27]
+    loads = [
+        pltpu.make_async_copy(source, local[i], sems.at[i]) for i, source in enumerate(sources)
+    ]
+    for load in loads:
+        load.start()
+    r24 = NY * r6
+    rows = out.shape[0]
+    out[...] = jnp.zeros_like(out)
+    vec[...] = jnp.zeros_like(vec)
+    for load in loads:
+        load.wait()
+    wq, wo, wf, wp, g1, b1, qv, ob, g2, b2, fb, pb = local
+    out[0:r6, 0 : 3 * D] = wq[...]
+    out[0:r6, 3 * D : 4 * D] = wo[...]
+    value = wf[...].astype(F32)
+    for natural, packed in hidden_order(count, r24):
+        wide[:, packed : packed + r24] = value[:, natural : natural + r24]
+    out[0:r6, 4 * D : 4 * D + FF] = wide[...].astype(BF16)
+    value = wp[...].astype(F32)
+    for i in range(r24 // rows):
+        at = 4 * D + FF + i * D
+        out[:, at : at + D] = value[i * rows : (i + 1) * rows, :].astype(BF16)
+    vec[0:1, 0:r6] = g1[...].astype(F32)
+    vec[1:2, 0:r6] = b1[...].astype(F32)
+    both = qv[...].astype(F32)
+    vec[2:3, 0:r6] = both[:, 0:r6]
+    vec[3:4, 0:r6] = both[:, r6 : 2 * r6]
+    vec[4:5, 0:r6] = ob[...].astype(F32)
+    vec[5:6, 0:r6] = g2[...].astype(F32)
+    vec[6:7, 0:r6] = b2[...].astype(F32)
+    vec[7:8, 0:r6] = pb[...].astype(F32)
+    hidden = fb[...].astype(F32)
+    for i in range(r24 // rows):
+        vec[8 + i : 9 + i, 0:rows] = hidden[:, i * rows : (i + 1) * rows]
+    at = out.shape[1] - 128
+    out[:, at : at + 128] = jnp.transpose(vec[...])[0:rows, :].astype(BF16)
+
+
+def turns_kernel(n, base, meta, *refs):
+    parts, outs, total = refs[: -n - 1], refs[-n - 1 : -1], refs[-1]
+    value = parts[0][...].astype(F32)
+    for part in parts[1:]:
+        value = value + part[...].astype(F32)
+    total[...] = value
+    size = total.shape[0] // n
+    for k in range(n):
+        at = lax.rem(meta[base] + k, n) * size
+        outs[k][...] = total[pl.ds(at, size)].astype(BF16)
+
+
+def rows_kernel(n, r6, meta, *refs):
+    parts, outs = refs[:n], refs[n:]
+    total = parts[0][...].astype(F32)
+    for part in parts[1:]:
+        total = total + part[...].astype(F32)
+    y = meta[M_ZXY + 2]
+    r24, width = total.shape
+    rows = outs[0].shape[0]
+    i = lax.broadcasted_iota(jnp.int32, (rows, r24), 0)
+    j = lax.broadcasted_iota(jnp.int32, (rows, r24), 1)
+    lane = lax.broadcasted_iota(jnp.int32, (rows, 128), 1)
+    value = total.astype(BF16)
+    bias = value[:, D : D + 128]
+    for k in range(NY):
+        to = lax.rem(y + k, NY)
+        chosen = jnp.where((i < r6) & (j == i + to * r6), 1.0, 0.0).astype(BF16)
+        outs[k][:, 0:width] = dot_nn(chosen, value).astype(BF16)
+        hidden = jnp.zeros((rows, 128), F32)
+        for g in range(r24 // rows):
+            group = dot_nn(jnp.where(j == i + g * rows, 1.0, 0.0).astype(BF16), bias)
+            column = jnp.sum(jnp.where(lane == 8 + to, group, 0.0), axis=1, keepdims=True)
+            hidden = hidden + jnp.where(lane == g, column, 0.0)
+        outs[k][:, width : width + 128] = hidden.astype(BF16)
+
+
+def split_kernel(r6, meta, reduced, *refs):
+    outs, (blocks,) = refs[:NY], refs[NY:]
+    r24 = NY * r6
+    rows = outs[0].shape[0]
+    y = meta[M_ZXY + 2]
+    for q in range(NY):
+        blocks[q] = reduced[:, FF + q * D : FF + (q + 1) * D].astype(F32)
+    i = lax.broadcasted_iota(jnp.int32, (rows, r24), 0)
+    j = lax.broadcasted_iota(jnp.int32, (rows, r24), 1)
+    for k in range(NY):
+        to = lax.rem(y + k, NY)
+        chosen = jnp.where((i < r6) & (j == i + to * r6), 1.0, 0.0).astype(BF16)
+        outs[k][:, 0:FF] = dot_nn(chosen, reduced[:, 0:FF]).astype(BF16)
+        value = blocks[to]
+        for n in range(r24 // rows):
+            outs[k][:, FF + n * D : FF + (n + 1) * D] = value[n * rows : (n + 1) * rows, :].astype(
+                BF16
+            )
+
+
+def join_kernel(count, r6, *refs):
+    parts, (fc, proj) = refs[:NY], refs[NY:]
+    r24 = NY * r6
+    rows = parts[0].shape[0]
+    total = parts[0][...].astype(F32)
+    for k in range(1, NY):
+        total = total + parts[k][...].astype(F32)
+    for natural, packed in hidden_order(count, r24):
+        fc[:, natural : natural + r24] = total[0:r6, packed : packed + r24]
+    for n in range(r24 // rows):
+        proj[n * rows : (n + 1) * rows, :] = total[:, FF + n * D : FF + (n + 1) * D]
+
+
+def back_kernel(nc, meta, *refs):
     do_refs, refs = refs[:NY], refs[NY:]
     x_refs, refs = refs[:NY], refs[NY:]
-    qkv_ref, lse_ref, a1_ref, w_ref, r0_ref, k_ref = refs[:6]
-    dh_refs, refs = refs[6 : 6 + NY], refs[6 + NY :]
-    gq_ref, doh, dq, dk, dv, dqkv, dh, gvec = refs
+    qkv_ref, lse_ref, a1_ref, w_ref, r0_ref, k_ref, rest = refs[:7]
+    dh_refs, refs = refs[7 : 7 + NY], refs[7 + NY :]
+    halves, refs = refs[:nc], refs[nc:]
+    doh, dq, dk, dv, dqkv, dh, gvec, gq_ref = refs
     y = meta[M_ZXY + 2]
     for k in range(NY):
         for j in range(SLOTS):
@@ -324,11 +433,18 @@
 
     def grads(c, carry):
         rows = pl.ds(pl.multiple_of(c * 256, 256), 256)
-        gq_ref[rows, 0:WQ] = dot_tn(a1_ref[:, rows], dqkv[...]).astype(BF16)
+        gq_ref[rows, D + 128 : D + 128 + WQ] = dot_tn(a1_ref[:, rows], dqkv[...])
         return carry
 
     lax.fori_loop(0, 3, grads, 0)
-    gq_ref[:, WQ:QCOLS] = jnp.transpose(gvec[...])[:, 64:128].astype(BF16)
+    gq_ref[:, 0 : D + 128] = rest[...].astype(F32)
+    gq_ref[:, D + 128 + WQ :] = jnp.transpose(gvec[...])[:, 64:128]
+    blocks, size = halves[0].shape[:2]
+    for k in range(nc):
+        core = lax.rem(meta[M_CORE] + k, nc) * size
+        for i in range(blocks):
+            at = pl.multiple_of(i * size * nc + core, 8)
+            halves[k][i] = gq_ref[pl.ds(at, size), :].astype(BF16)
 
 
 def end_kernel(*refs):
@@ -350,7 +466,7 @@
 
 VMEM = pl.BlockSpec(memory_space=pltpu.VMEM)
 SMEM = pl.BlockSpec(memory_space=pltpu.SMEM)
-ANY = pl.BlockSpec(memory_space=pl.ANY)
+HBM = pl.BlockSpec(memory_space=pltpu.HBM)
 
 
 def cost(flops, nbytes):
@@ -416,40 +532,54 @@
     limits = jnp.sum(jnp.where(short, (seqs * SEQ_STRIDE + lens)[None, :], 0), axis=1)
     place = jnp.stack([z, x, y]).astype(jnp.int32)
     alive = (lens - blocks * BLK)[:SLOTS]
-    meta = jnp.concatenate([inverse, codes, bases, limits, place, alive, jnp.zeros((2,), jnp.int32)])
+    core = jnp.stack([c, jnp.zeros_like(c)]).astype(jnp.int32)
+    meta = jnp.concatenate([inverse, codes, bases, limits, place, alive, core])
     lane = np.arange(HW)
     r0 = jnp.asarray(((lane // (2 * r6)) * r6 + lane % r6)[None, :], jnp.int32)
     kk = jnp.asarray(((lane // r6) % 2)[None, :], jnp.int32)
 
-    token_parts = [tokens] + [shift_y(tokens, k) for k in range(1, NY)]
-    vec = jnp.concatenate(
+    rows8 = (r6 + 7) // 8 * 8
+    groups = r24 // rows8
+    width = 4 * D + FF + groups * D + 128
+    vectors = (ln1_gain, ln1_bias, qv_bias, out_bias, ln2_gain, ln2_bias, feed_input_bias, proj_bias)
+    sources = [w_qkv, w_out, w_fc, w_proj] + [v[None, :] for v in vectors]
+    payload = pl.pallas_call(
+        lambda *refs: pack_kernel(count, r6, *refs),
+        in_specs=[HBM] * 12,
+        out_specs=VMEM,
+        out_shape=jax.ShapeDtypeStruct((rows8, width), BF16),
+        scratch_shapes=[pltpu.VMEM((r6, FF), F32), pltpu.VMEM((128, max(128, rows8)), F32)]
+        + [pltpu.VMEM(v.shape, BF16) for v in sources]
+        + [pltpu.SemaphoreType.DMA((12,))],
+        compiler_params=params(60),
+        name="pack",
+    )(*sources)
+    payloads = [payload] + [shift_y(payload, k) for k in range(1, NY)]
+    later, _ = lax.optimization_barrier((tokens, payload))
+    token_parts = [tokens] + [shift_y(later, k) for k in range(1, NY)]
+    spread = jnp.stack(payloads)
+    spread = jnp.concatenate([pick(spread, (y - q) % NY)[None] for q in range(NY)])
+    v0 = width - 128
+    vec_rows = spread[:, :r6, v0 : v0 + 8].reshape(r24, 8)
+    qkv_mine = pick(spread[:, :r6, : 3 * D].reshape(r24, 3, NY, HW), y, 2).reshape(r24, WQ)
+    wq_local = jnp.concatenate([qkv_mine, vec_rows, jnp.zeros((r24, 56), BF16)], axis=1)
+    proj_rows = jnp.concatenate(
         [
-            ln1_gain[:, None],
-            ln1_bias[:, None],
-            qv_bias.reshape(2, r6).T,
-            out_bias[:, None],
-            ln2_gain[:, None],
-            ln2_bias[:, None],
-            proj_bias[:, None],
-            feed_input_bias.reshape(r6, 4),
-            jnp.zeros((r6, 116), BF16),
+            jnp.concatenate(
+                [
+                    spread[q, :, 4 * D + FF + n * D : 4 * D + FF + (n + 1) * D]
+                    for n in range(groups)
+                ],
+                axis=0,
+            )
+            for q in range(NY)
         ],
         axis=1,
     )
-    fc_local = w_fc.reshape(r6, count, 4, r24).transpose(0, 2, 1, 3).reshape(r6, FF)
-    payload = jnp.concatenate([w_qkv, w_out, fc_local, w_proj.reshape(r6, 4 * D), vec], axis=1)
-    spread = lax.all_gather(payload, "seq", axis=0, tiled=False)
-    v0 = 3 * D + D + 2 * FF
-    vec_rows = spread[:, :, v0 : v0 + 8].reshape(r24, 8)
-    qkv_mine = pick(spread[:, :, : 3 * D].reshape(r24, 3, NY, HW), y, 2).reshape(r24, WQ)
-    wq_local = jnp.concatenate([qkv_mine, vec_rows, jnp.zeros((r24, 56), BF16)], axis=1)
-    proj_rows = (
-        spread[:, :, 4 * D + FF : v0].reshape(NY, r24, D).transpose(1, 0, 2).reshape(r24, NY * D)
-    )
-    fcb_rows = spread[:, :, v0 + 8 : v0 + 12].reshape(NY, r24).T
+    fcb_rows = jnp.transpose(spread[:, :, v0 + 8 : v0 + 8 + groups], (2, 1, 0)).reshape(r24, NY)
     w_local = jnp.concatenate(
         [
-            spread[:, :, 3 * D : 4 * D + FF].reshape(r24, D + FF),
+            spread[:, :r6, 3 * D : 4 * D + FF].reshape(r24, D + FF),
             proj_rows,
             vec_rows,
             fcb_rows,
@@ -480,7 +610,7 @@
         + [jax.ShapeDtypeStruct((ROWS, HW), BF16)] * NY
         + [jax.ShapeDtypeStruct((D, QCOLS), BF16), jax.ShapeDtypeStruct((8, D), F32)],
         scratch_shapes=[pltpu.VMEM((HEADS, GROWS, HD), F32)],
-        compiler_params=params(48),
+        compiler_params=params(60),
         cost_estimate=cost(8e9, 15e6),
         name="front",
     )(meta, *token_parts, *planes, r0, kk)
@@ -489,45 +619,49 @@
     wq, gain_one = front[3 + NY :]
 
     mixed_parts = [mixed[0]] + [shift_y(mixed[NY - k], k) for k in range(1, NY)]
+    wide32 = jax.ShapeDtypeStruct((ROWS, D), F32)
+    wide16 = jax.ShapeDtypeStruct((ROWS, D), BF16)
     middle = pl.pallas_call(
         middle_kernel,
-        in_specs=[SMEM] + [VMEM] * (NY + 2) + [ANY],
-        out_specs=[VMEM] * (2 + NY) + [ANY],
-        out_shape=[jax.ShapeDtypeStruct((ROWS, D), BF16), jax.ShapeDtypeStruct((ROWS, D), F32)]
+        in_specs=[SMEM] + [VMEM] * (NY + 2) + [HBM],
+        out_specs=[VMEM] * (3 + NY) + [HBM],
+        out_shape=[wide16, wide32]
         + [jax.ShapeDtypeStruct((ROWS, HW), BF16)] * NY
-        + [jax.ShapeDtypeStruct((D, WCOLS), BF16)],
+        + [
+            jax.ShapeDtypeStruct((D, D + 128), BF16),
+            jax.ShapeDtypeStruct((D, 8 * D), BF16),
+        ],
         scratch_shapes=[
-            pltpu.VMEM((D, WCOLS), BF16),
-            pltpu.VMEM((D, WCOLS), BF16),
+            pltpu.VMEM((D, 9 * D + 128), BF16),
+            pltpu.VMEM((D, 8 * D), BF16),
+            pltpu.VMEM((D, D), F32),
+            pltpu.VMEM((ROWS, D), F32),
+            pltpu.VMEM((ROWS, D), BF16),
+            pltpu.VMEM((ROWS, D), BF16),
+            pltpu.VMEM((D, ROWS), BF16),
             pltpu.VMEM((ROWS, D), F32),
             pltpu.VMEM((ROWS, D), F32),
-            pltpu.VMEM((ROWS, 1), F32),
-            pltpu.VMEM((ROWS, D), BF16),
-            pltpu.VMEM((D, ROWS), BF16),
-            pltpu.VMEM((ROWS, D), BF16),
-            pltpu.VMEM((ROWS, D), F32),
-            pltpu.VMEM((ROWS, D), F32),
-            pltpu.VMEM((12, 8, 256), F32),
             pltpu.VMEM((128, D), F32),
-            pltpu.SemaphoreType.DMA((8,)),
+            pltpu.SemaphoreType.DMA((18,)),
         ],
-        compiler_params=params(52),
+        compiler_params=params(60),
         cost_estimate=cost(13e9, 28e6),
         name="middle",
     )(meta, *mixed_parts, tokens, cotangent, weights)
     block_out, middle_grad = middle[:2]
     do_made = middle[2 : 2 + NY]
-    reduced = lax.psum_scatter(middle[2 + NY], "fsdp", scatter_dimension=0, tiled=True)
-    reduced = lax.optimization_barrier(reduced)
+    reduced_a = lax.psum_scatter(middle[3 + NY], "fsdp", scatter_dimension=0, tiled=True)
+    reduced_a = lax.optimization_barrier(reduced_a)
 
     do_parts = [do_made[0]] + [shift_y(do_made[NY - k], k) for k in range(1, NY)]
+    rest_cols = D + 128 + QCOLS
     back = pl.pallas_call(
-        back_kernel,
-        in_specs=[SMEM] + [VMEM] * (2 * NY + 6),
-        out_specs=[VMEM] * (NY + 1),
+        lambda *refs: back_kernel(nc, *refs),
+        in_specs=[SMEM] + [VMEM] * (2 * NY + 7),
+        out_specs=[VMEM] * (NY + nc),
         out_shape=[jax.ShapeDtypeStruct((ROWS, D), F32)]
         + [jax.ShapeDtypeStruct((ROWS, D), BF16)] * (NY - 1)
-        + [jax.ShapeDtypeStruct((D, QCOLS), BF16)],
+        + [jax.ShapeDtypeStruct((nz * nx, r24, rest_cols), BF16)] * nc,
         scratch_shapes=[
             pltpu.VMEM((HEADS, GROWS, HD), BF16),
             pltpu.VMEM((HEADS, GROWS, HD), F32),
@@ -536,13 +670,52 @@
             pltpu.VMEM((GROWS, WQ), BF16),
             pltpu.VMEM((GROWS, D), F32),
             pltpu.VMEM((128, D), F32),
+            pltpu.VMEM((D, rest_cols), F32),
         ],
-        compiler_params=params(56),
+        compiler_params=params(60),
         cost_estimate=cost(12e9, 20e6),
         name="back",
-    )(meta, *do_parts, *token_parts, qkv, lse, acts, wq, r0, kk)
+    )(meta, *do_parts, *token_parts, qkv, lse, acts, wq, r0, kk, middle[2 + NY])
     dh_made = back[:NY]
     dh_parts = [dh_made[0]] + [shift_y(dh_made[NY - k], k) for k in range(1, NY)]
+
+    def turns(parts, n, base, size):
+        total = parts[0].shape
+        return pl.pallas_call(
+            lambda *refs: turns_kernel(n, base, *refs),
+            in_specs=[SMEM] + [VMEM] * len(parts),
+            out_specs=[VMEM] * n,
+            out_shape=[jax.ShapeDtypeStruct((total[0] // n,) + total[1:], BF16)] * n,
+            scratch_shapes=[pltpu.VMEM(total, F32)],
+            compiler_params=params(24),
+            name="turns",
+        )(meta, *parts)
+
+    parts = [back[NY]]
+    if nc == 2:
+        parts.append(shift_f(back[NY + 1], 0, 0, 1))
+    made = turns(parts, nz, M_ZXY, nx)
+    parts = [made[0]] + [shift_f(made[k], k, 0, 0) for k in range(1, nz)]
+    parts, dh_parts = lax.optimization_barrier((parts, dh_parts))
+    made = turns(parts, nx, M_ZXY + 1, 1)
+    parts = [made[0]] + [shift_f(made[k], 0, k, 0) for k in range(1, nx)]
+    made = pl.pallas_call(
+        lambda *refs: rows_kernel(nx, r6, *refs),
+        in_specs=[SMEM] + [VMEM] * nx,
+        out_specs=[VMEM] * NY,
+        out_shape=[jax.ShapeDtypeStruct((rows8, rest_cols + 128), BF16)] * NY,
+        compiler_params=params(16),
+        name="rows",
+    )(meta, *[part[0] for part in parts])
+    row_parts = [made[0]] + [shift_y(made[k], k) for k in range(1, NY)]
+    c_heads = D + 128
+    summed = sum(part.astype(F32) for part in row_parts)
+    heads = jnp.stack([part[:r6, c_heads : c_heads + WQ] for part in row_parts])
+    heads = jnp.concatenate([pick(heads, (y - q) % NY)[:, None] for q in range(NY)], axis=1)
+    grad_qkv = heads.reshape(r6, NY, 3, HW).transpose(0, 2, 1, 3).reshape(r6, 3 * D).astype(F32)
+    vecs = summed[:r6, D : D + 8]
+    tail = summed[:r6, c_heads + WQ : c_heads + WQ + 4]
+    grad_fcb = summed[:, rest_cols : rest_cols + groups].T.reshape(r24)
     tokens_grad = pl.pallas_call(
         end_kernel,
         in_specs=[VMEM] * (NY + 3),
@@ -553,54 +726,39 @@
         name="end",
     )(*dh_parts, tokens, middle_grad, gain_one)
 
-    def exchange(value, i, n, send):
-        total = pick(value, i).astype(F32)
-        for k in range(1, n):
-            total = total + send(pick(value, (i + k) % n), k).astype(F32)
-        return total.astype(BF16)
-
-    gq = back[NY].reshape(nz, nx, nc, r24, QCOLS)
-    if nc == 2:
-        kept = pick(gq, c, 2).astype(F32)
-        gq = (kept + shift_f(pick(gq, 1 - c, 2), 0, 0, 1).astype(F32)).astype(BF16)
-    else:
-        gq = gq[:, :, 0]
-    gq = exchange(gq, z, nz, lambda v, k: shift_f(v, k, 0, 0))
-    gq = exchange(gq, x, nx, lambda v, k: shift_f(v, 0, k, 0))
-
-    row_part = jnp.concatenate(
-        [reduced[:, :C_PROJ], reduced[:, C_VEC : C_VEC + 8], gq[:, WQ : WQ + 8], gq[:, :WQ]], axis=1
-    ).reshape(NY, r6, C_PROJ + 16 + WQ)
-    proj_part = jnp.concatenate([reduced[:, C_PROJ:C_VEC].reshape(r24, NY, D)], axis=0)
-    proj_part = jnp.transpose(proj_part, (1, 0, 2))
-    fcb_part = jnp.pad(reduced[:, C_VEC + 8 : C_VEC + 12].T[:, :, None], ((0, 0), (0, 0), (0, 127)))
-    proj_part = jnp.concatenate([proj_part, fcb_part], axis=2)
-    row_parts = [pick(row_part, y)]
-    proj_parts = [pick(proj_part, y)]
-    for k in range(1, NY):
-        row_parts.append(shift_y(pick(row_part, (y + k) % NY), k))
-        proj_parts.append(shift_y(pick(proj_part, (y + k) % NY), k))
-    rows_sum = sum(part[:, : C_PROJ + 16].astype(F32) for part in row_parts)
-    proj_sum = sum(part.astype(F32) for part in proj_parts)
-    heads = jnp.stack([part[:, C_PROJ + 16 :] for part in row_parts])
-    heads = jnp.concatenate([pick(heads, (y - q) % NY)[:, None] for q in range(NY)], axis=1)
-    grad_qkv = heads.reshape(r6, NY, 3, HW).transpose(0, 2, 1, 3).reshape(r6, 3 * D).astype(F32)
-    grad_fc = rows_sum[:, C_FC:C_PROJ].reshape(r6, NY, count, r24).transpose(0, 2, 1, 3)
-    vecs = rows_sum[:, C_PROJ:]
+    packed = jax.ShapeDtypeStruct((rows8, FF + groups * D), BF16)
+    parts = pl.pallas_call(
+        lambda *refs: split_kernel(r6, *refs),
+        in_specs=[SMEM, VMEM],
+        out_specs=[VMEM] * NY,
+        out_shape=[packed] * NY,
+        scratch_shapes=[pltpu.VMEM((NY, r24, D), F32)],
+        compiler_params=params(60),
+        name="split",
+    )(meta, reduced_a)
+    parts = [parts[0]] + [shift_y(parts[k], k) for k in range(1, NY)]
+    grad_fc, grad_proj = pl.pallas_call(
+        lambda *refs: join_kernel(count, r6, *refs),
+        in_specs=[VMEM] * NY,
+        out_specs=[VMEM] * 2,
+        out_shape=[jax.ShapeDtypeStruct((r6, FF), F32), jax.ShapeDtypeStruct((r24, D), F32)],
+        compiler_params=params(16),
+        name="join",
+    )(*parts)
     return (
         block_out,
         tokens_grad,
-        vecs[:, 8],
-        vecs[:, 9],
+        tail[:, 0],
+        tail[:, 1],
         grad_qkv,
-        vecs[:, 10:12].T.reshape(2 * r6),
-        rows_sum[:, :D],
+        tail[:, 2:4].T.reshape(2 * r6),
+        summed[:r6, :D],
         vecs[:, 4],
         vecs[:, 5],
         vecs[:, 6],
-        grad_fc.reshape(r6, FF),
-        proj_sum[:, D],
-        proj_sum[:, :D],
+        grad_fc,
+        grad_fcb,
+        grad_proj,
         vecs[:, 7],
     )
 

time: 267 us -> 261 us (0.978)
  local copies, waits for them, and re-layouts: 30.2 us -> 11.7 us
  blocking collectives: 13.7 us -> 0 us
  Pallas kernels: 79.6 us -> 91.5 us
  waiting for transfers between devices: 72.2 us -> 81.9 us
  starting transfers between devices: 51.8 us -> 56 us
    unnamed x3 -> x2, waiting for transfers between devices: 20.2 us -> 0.03 us
    ppermute x18 -> x21, waiting for transfers between devices: 28.7 us -> 44.8 us  [shift_y(): return lax.ppermute(value, 'seq', [(i, (i + k) % NY) for i in range(NY)])]
    all_gather x1 -> x0, blocking collectives: 13.7 us -> none  [on_device(): spread = lax.all_gather(payload, 'seq', axis=0, tiled=False)]
    pallas_call x2 -> x8, Pallas kernels: 58.2 us -> 69.8 us  [the longest x1 33.9 us: on_device(): pl.pallas_call(middle_kernel, in_specs=[SMEM] + [VMEM] * (NY + 2) + [HBM]...]
    ppermute x14, waiting for transfers between devices: 23.2 us -> 30.2 us  [shift_f(): return lax.ppermute(value, 'fsdp', pairs)]
    reduce_scatter x0 -> x1, waiting for transfers between devices: none -> 6.78 us  [on_device(): lax.psum_scatter(middle[3 + NY], 'fsdp', scatter_dimension=0, tiled=True)]
    reshape x18 -> x7, local copies, waits for them, and re-layouts: 6.35 us -> 1.7 us  [the longest x1 0.6 us: on_device(): grad_fcb = summed[:, rest_cols:rest_cols + groups].T.reshape(r24)]
    broadcast_in_dim x7 -> x0, local copies, waits for them, and re-layouts: 4.53 us -> none  [the longest x1 0.75 us: on_device(): ln2_gain[:, None]]
  transfers between devices with their start and end apart: 34 -> 37, of which waited for: 17 -> 22; matrix products, arithmetic and copies ran while one was open for 3% -> 2% of each run, Pallas kernels for 18% -> 21%
where the time goes in v2:
time: 261 us; the launch traced here: 258 us
  Pallas kernels  91.5 us (35%)
  waiting for transfers between devices  81.9 us (31%)
  starting transfers between devices  56 us (21%)
  between operations  14.8 us (6%)
  local copies, waits for them, and re-layouts  11.7 us (4%)
    ppermute x21, waiting for transfers between devices, shift_y(): return lax.ppermute(value, 'seq', [(i, (i + k) % NY) for i in range(NY)])  44.8 us
    pallas_call x1, Pallas kernels, on_device(): pl.pallas_call(middle_kernel, in_specs=[SMEM] + [VMEM] * (NY + 2) + [HBM]...  33.9 us
    ppermute x21, starting transfers between devices, shift_y(): return lax.ppermute(value, 'seq', [(i, (i + k) % NY) for i in range(NY)])  31 us
    ppermute x14, waiting for transfers between devices, shift_f(): return lax.ppermute(value, 'fsdp', pairs)  30.2 us
    pallas_call x1, Pallas kernels, on_device(): pl.pallas_call(lambda *refs: back_kernel(nc, *refs), in_specs=[SMEM] + [V...  28.7 us
    ppermute x14, starting transfers between devices, shift_f(): return lax.ppermute(value, 'fsdp', pairs)  24.9 us
    pallas_call x1, Pallas kernels, on_device(): pl.pallas_call(lambda *refs: front_kernel(nz, nx, *refs), in_specs=[SMEM]...  20 us
    reduce_scatter x1, waiting for transfers between devices, on_device(): lax.psum_scatter(middle[3 + NY], 'fsdp', scatter_dimension=0, tiled=True)  6.78 us
  transfers between devices with their start and end apart: 37, of which 22 were waited for; matrix products, arithmetic and copies ran while one was open for 2% of the time, Pallas kernels for 21%

profile of v2, /device:TPU:0, one launch (start us, length us, event | category | flops | bytes accessed | tf_op | source)
XLA Modules:
  0.0 258.0 jit_solution(15573640176380446376)
XLA Ops:
  9.1 3.2 %collective-permute-start.5 = (bf16[8,8576]{1,0:T(8,128)(2,1)}, bf16[8,8576]{1,0:T(8,128)(2,1)S(1)}, u32[]{:S(2)}, u32[]{:S(2)}) collective-permute-start(bf16[8,8576]{1,0:T(8,128)(2,1)} %pack.1), channel_id=1, source_target_pairs={{0,3},{1,0},{2,1},{3,2},{4,7},{5,4},{6,5},{7,6},{8,11},{9,8},{10,9... | collective-permute-start | bytes 411656 | tf_op jit(solution)/shard_map/ppermute | solution.py:506
  13.8 4.5 %collective-permute-done.5 = bf16[8,8576]{1,0:T(8,128)(2,1)S(1)} collective-permute-done((bf16[8,8576]{1,0:T(8,128)(2,1)}, bf16[8,8576]{1,0:T(8,128)(2,1)S(1)}, u32[]{:S(2)}, u32[]{:S(2)}) %collective-permute-start.5) | collective-permute-done | bytes 137248 | tf_op jit(solution)/shard_map/ppermute | solution.py:506
  26.6 3.1 %collective-permute-start.8 = (bf16[48,640]{1,0:T(8,128)(2,1)S(1)}, bf16[48,640]{1,0:T(8,128)(2,1)S(1)}, u32[]{:S(2)}, u32[]{:S(2)}) collective-permute-start(bf16[48,640]{1,0:T(8,128)(2,1)S(1)} %get-tuple-element.142), channel_id=1, source_target_pairs={{0,16},{4,20},{8,24},{12,28},{16,0},{20,4},{24,8},{28,12},{32,48},... | collective-permute-start | bytes 184328 | tf_op jit(solution)/shard_map/ppermute | solution.py:514
  30.2 2.6 %collective-permute-start.9 = (bf16[48,640]{1,0:T(8,128)(2,1)S(1)}, bf16[48,640]{1,0:T(8,128)(2,1)S(1)}, u32[]{:S(2)}, u32[]{:S(2)}) collective-permute-start(bf16[48,640]{1,0:T(8,128)(2,1)S(1)} %get-tuple-element.142), channel_id=1, source_target_pairs={{0,24},{4,28},{8,0},{12,4},{16,8},{20,12},{24,16},{28,20},{32,56},... | collective-permute-start | bytes 184328 | tf_op jit(solution)/shard_map/ppermute | solution.py:514
  35.1 4.5 %collective-permute-start.12 = (bf16[4,48,640]{2,1,0:T(8,128)(2,1)S(1)}, bf16[4,48,640]{2,1,0:T(8,128)(2,1)S(1)}, u32[]{:S(2)}, u32[]{:S(2)}) collective-permute-start(bf16[4,48,640]{2,1,0:T(8,128)(2,1)S(1)} %pad_maximum_fusion.2.refs_5_), channel_id=1, source_target_pairs={{0,96},{4,100},{8,104},{12,108},{16,112},{20,116},{24,120},{28,124... | collective-permute-start | bytes 737288 | tf_op jit(solution)/shard_map/ppermute | solution.py:514
  40.0 12.0 %collective-permute-done.12.refs_8_ = bf16[4,48,640]{2,1,0:T(8,128)(2,1)S(1)} collective-permute-done((bf16[4,48,640]{2,1,0:T(8,128)(2,1)S(1)}, bf16[4,48,640]{2,1,0:T(8,128)(2,1)S(1)}, u32[]{:S(2)}, u32[]{:S(2)}) %collective-permute-start.12) | collective-permute-done | bytes 245792 | tf_op jit(solution)/shard_map/ppermute | solution.py:514
  53.0 6.9 %collective-permute-done.10.refs_6_ = bf16[4,48,640]{2,1,0:T(8,128)(2,1)S(1)} collective-permute-done((bf16[4,48,640]{2,1,0:T(8,128)(2,1)S(1)}, bf16[4,48,640]{2,1,0:T(8,128)(2,1)S(1)}, u32[]{:S(2)}, u32[]{:S(2)}) %collective-permute-start.10) | collective-permute-done | bytes 245792 | tf_op jit(solution)/shard_map/ppermute | solution.py:514
  62.7 20.0 %front.1 = (bf16[1536,768]{1,0:T(8,128)(2,1)}, bf16[9,1536,64]{2,1,0:T(8,128)(2,1)}, f32[3,1536,1]{2,1,0:T(8,128)}, bf16[384,192]{1,0:T(8,128)(2,1)}, bf16[384,1...) custom-call(s32[32]{0:T(128)} %concatenate.39.refs_0_.meta, ...), custom_call_target="tpu_custom_call" | custom-call | flops 8000000000 | bytes 15000000 | tf_op jit(solution)/shard_map/front/pallas_call | solution.py:601
  83.6 2.7 %collective-permute-start.14 = (bf16[384,192]{1,0:T(8,128)(2,1)}, bf16[384,192]{1,0:T(8,128)(2,1)S(1)}, u32[]{:S(2)}, u32[]{:S(2)}) collective-permute-start(bf16[384,192]{1,0:T(8,128)(2,1)} %get-tuple-element.67), channel_id=1, source_target_pairs={{0,2},{1,3},{2,0},{3,1},{4,6},{5,7},{6,4},{7,5},{8,10},{9,11},{10,... | collective-permute-start | bytes 442376 | tf_op jit(solution)/shard_map/ppermute | solution.py:506
  88.6 6.6 %collective-permute-done.13.refs_1_ = bf16[384,192]{1,0:T(8,128)(2,1)S(1)} collective-permute-done((bf16[384,192]{1,0:T(8,128)(2,1)}, bf16[384,192]{1,0:T(8,128)(2,1)S(1)}, u32[]{:S(2)}, u32[]{:S(2)}) %collective-permute-start.13) | collective-permute-done | bytes 147488 | tf_op jit(solution)/shard_map/ppermute | solution.py:506
  96.7 33.9 %middle.1 = (bf16[384,768]{1,0:T(8,128)(2,1)}, f32[384,768]{1,0:T(8,128)}, bf16[384,192]{1,0:T(8,128)(2,1)}, bf16[384,192]{1,0:T(8,128)(2,1)}, bf16[384,192]{1,0...) custom-call(s32[32]{0:T(128)} %concatenate.39.refs_0_.meta, ...), custom_call_target="tpu_custom_call" | custom-call | flops 12999999488 | bytes 28000000 | tf_op jit(solution)/shard_map/middle/pallas_call | solution.py:624
  131.9 3.6 %collective-permute-start.17 = (bf16[384,192]{1,0:T(8,128)(2,1)S(1)}, bf16[384,192]{1,0:T(8,128)(2,1)S(1)}, u32[]{:S(2)}, u32[]{:S(2)}) collective-permute-start(bf16[384,192]{1,0:T(8,128)(2,1)S(1)} %copy-done.22), channel_id=1, source_target_pairs={{0,2},{1,3},{2,0},{3,1},{4,6},{5,7},{6,4},{7,5},{8,10},{9,11},{10,... | collective-permute-start | bytes 442376 | tf_op jit(solution)/shard_map/ppermute | solution.py:506
  135.5 3.4 %collective-permute-done.16.refs_2_ = bf16[384,192]{1,0:T(8,128)(2,1)S(1)} collective-permute-done((bf16[384,192]{1,0:T(8,128)(2,1)S(1)}, bf16[384,192]{1,0:T(8,128)(2,1)S(1)}, u32[]{:S(2)}, u32[]{:S(2)}) %collective-permute-start.16) | collective-permute-done | bytes 147488 | tf_op jit(solution)/shard_map/ppermute | solution.py:506
  138.9 5.2 %collective-permute-done.17.refs_3_ = bf16[384,192]{1,0:T(8,128)(2,1)S(1)} collective-permute-done((bf16[384,192]{1,0:T(8,128)(2,1)S(1)}, bf16[384,192]{1,0:T(8,128)(2,1)S(1)}, u32[]{:S(2)}, u32[]{:S(2)}) %collective-permute-start.17) | collective-permute-done | bytes 147488 | tf_op jit(solution)/shard_map/ppermute | solution.py:506
  144.9 28.7 %back.1 = (f32[384,768]{1,0:T(8,128)}, bf16[384,768]{1,0:T(8,128)(2,1)}, bf16[384,768]{1,0:T(8,128)(2,1)}, bf16[384,768]{1,0:T(8,128)(2,1)}, bf16[16,24,1536]{2,...) custom-call(s32[32]{0:T(128)} %concatenate.39.refs_0_.meta, bf16[384,192]{1,0:T(8,128)(2,1)} %get-tuple-element.70.refs_1_, ...), custom_call_target="tpu_custom_call" | custom-call | flops 12000000000 | bytes 20000000 | tf_op jit(solution)/shard_map/back/pallas_call | solution.py:658
  173.6 3.5 %collective-permute-start.24 = (bf16[384,768]{1,0:T(8,128)(2,1)}, bf16[384,768]{1,0:T(8,128)(2,1)S(1)}, u32[]{:S(2)}, u32[]{:S(2)}) collective-permute-start(bf16[384,768]{1,0:T(8,128)(2,1)} %get-tuple-element.87), channel_id=1, source_target_pairs={{0,2},{1,3},{2,0},{3,1},{4,6},{5,7},{6,4},{7,5},{8,10},{9,11},{10,... | collective-permute-start | bytes 1769480 | tf_op jit(solution)/shard_map/ppermute | solution.py:506
  179.5 2.6 %collective-permute-start.20 = (bf16[4,24,1536]{2,1,0:T(8,128)(2,1)S(1)}, bf16[4,24,1536]{2,1,0:T(8,128)(2,1)S(1)}, u32[]{:S(2)}, u32[]{:S(2)}) collective-permute-start(bf16[4,24,1536]{2,1,0:T(8,128)(2,1)S(1)} %get-tuple-element.82), channel_id=1, source_target_pairs={{0,32},{4,36},{8,40},{12,44},{16,48},{20,52},{24,56},{28,60},{32,6... | collective-permute-start | bytes 884744 | tf_op jit(solution)/shard_map/ppermute | solution.py:514
  182.1 3.4 %collective-permute-start.21 = (bf16[4,24,1536]{2,1,0:T(8,128)(2,1)S(1)}, bf16[4,24,1536]{2,1,0:T(8,128)(2,1)S(1)}, u32[]{:S(2)}, u32[]{:S(2)}) collective-permute-start(bf16[4,24,1536]{2,1,0:T(8,128)(2,1)S(1)} %get-tuple-element.83), channel_id=1, source_target_pairs={{0,64},{4,68},{8,72},{12,76},{16,80},{20,84},{24,88},{28,92},{32,9... | collective-permute-start | bytes 884744 | tf_op jit(solution)/shard_map/ppermute | solution.py:514
  185.5 5.3 %collective-permute-done.23.refs_1_ = bf16[384,768]{1,0:T(8,128)(2,1)S(1)} collective-permute-done((bf16[384,768]{1,0:T(8,128)(2,1)}, bf16[384,768]{1,0:T(8,128)(2,1)S(1)}, u32[]{:S(2)}, u32[]{:S(2)}) %collective-permute-start.23) | collective-permute-done | bytes 589856 | tf_op jit(solution)/shard_map/ppermute | solution.py:506
  190.8 4.5 %collective-permute-start.22 = (bf16[4,24,1536]{2,1,0:T(8,128)(2,1)S(1)}, bf16[4,24,1536]{2,1,0:T(8,128)(2,1)S(1)}, u32[]{:S(2)}, u32[]{:S(2)}) collective-permute-start(bf16[4,24,1536]{2,1,0:T(8,128)(2,1)S(1)} %get-tuple-element.84), channel_id=1, source_target_pairs={{0,96},{4,100},{8,104},{12,108},{16,112},{20,116},{24,120},{28,124... | collective-permute-start | bytes 884744 | tf_op jit(solution)/shard_map/ppermute | solution.py:514
  195.3 8.4 %collective-permute-done.24.refs_2_ = bf16[384,768]{1,0:T(8,128)(2,1)S(1)} collective-permute-done((bf16[384,768]{1,0:T(8,128)(2,1)}, bf16[384,768]{1,0:T(8,128)(2,1)S(1)}, u32[]{:S(2)}, u32[]{:S(2)}) %collective-permute-start.24) | collective-permute-done | bytes 589856 | tf_op jit(solution)/shard_map/ppermute | solution.py:506
  204.0 7.9 %collective-permute-done.21.refs_3_ = bf16[4,24,1536]{2,1,0:T(8,128)(2,1)S(1)} collective-permute-done((bf16[4,24,1536]{2,1,0:T(8,128)(2,1)S(1)}, bf16[4,24,1536]{2,1,0:T(8,128)(2,1)S(1)}, u32[]{:S(2)}, u32[]{:S(2)}) %collective-permute-start.21) | collective-permute-done | bytes 294944 | tf_op jit(solution)/shard_map/ppermute | solution.py:514
  231.6 6.8 %reduce-scatter.2.cloned.1.call-done.refs_1_ = bf16[24,6144]{1,0:T(8,128)(2,1)} async-done(((bf16[768,6144]{1,0:T(8,128)(2,1)}), bf16[24,6144]{1,0:T(8,128)(2,1)}) %reduce-scatter.2.cloned.1.call-update) | async-done | bytes 294928 | tf_op jit(solution)/shard_map/reduce_scatter | solution.py:653
  241.8 2.7 %collective-permute-start.33 = (bf16[8,5376]{1,0:T(8,128)(2,1)}, bf16[8,5376]{1,0:T(8,128)(2,1)S(1)}, u32[]{:S(2)}, u32[]{:S(2)}) collective-permute-start(bf16[8,5376]{1,0:T(8,128)(2,1)} %get-tuple-element.110), channel_id=1, source_target_pairs={{0,2},{1,3},{2,0},{3,1},{4,6},{5,7},{6,4},{7,5},{8,10},{9,11},{10,... | collective-permute-start | bytes 258056 | tf_op jit(solution)/shard_map/ppermute | solution.py:506
  (175 shorter events, 57.2 us)
Async XLA Ops:
  7.2 88.8 %all-gather.2.cloned.1.call-start = ((), (), s32[]{:S(2)}) async-start(), calls=%async_computation.1 | async-start | bytes 11151360 | tf_op jit(solution)/shard_map/all_gather | solution.py:590
  9.1 9.3 %collective-permute-start.5 = (bf16[8,8576]{1,0:T(8,128)(2,1)}, bf16[8,8576]{1,0:T(8,128)(2,1)S(1)}, u32[]{:S(2)}, u32[]{:S(2)}) collective-permute-start(bf16[8,8576]{1,0:T(8,128)(2,1)} %pack.1), channel_id=1, source_target_pairs={{0,3},{1,0},{2,1},{3,2},{4,7},{5,4},{6,5},{7,6},{8,11},{9,8},{10,9... | collective-permute-start | bytes 411656 | tf_op jit(solution)/shard_map/ppermute | solution.py:506
  12.2 8.3 %collective-permute-start.4 = (bf16[8,8576]{1,0:T(8,128)(2,1)}, bf16[8,8576]{1,0:T(8,128)(2,1)S(1)}, u32[]{:S(2)}, u32[]{:S(2)}) collective-permute-start(bf16[8,8576]{1,0:T(8,128)(2,1)} %pack.1), channel_id=1, source_target_pairs={{0,2},{1,3},{2,0},{3,1},{4,6},{5,7},{6,4},{7,5},{8,10},{9,11},{10,... | collective-permute-start | bytes 411656 | tf_op jit(solution)/shard_map/ppermute | solution.py:506
  12.8 9.1 %collective-permute-start.3 = (bf16[8,8576]{1,0:T(8,128)(2,1)}, bf16[8,8576]{1,0:T(8,128)(2,1)S(1)}, u32[]{:S(2)}, u32[]{:S(2)}) collective-permute-start(bf16[8,8576]{1,0:T(8,128)(2,1)} %pack.1), channel_id=1, source_target_pairs={{0,1},{1,2},{2,3},{3,0},{4,5},{5,6},{6,7},{7,4},{8,9},{9,10},{10,1... | collective-permute-start | bytes 411656 | tf_op jit(solution)/shard_map/ppermute | solution.py:506
  24.5 214.0 %reduce-scatter.2.cloned.1.call-start = ((), (), s32[]{:S(2)}) async-start(), calls=%async_computation.2 | async-start | bytes 9732096 | tf_op jit(solution)/shard_map/reduce_scatter | solution.py:653
  26.6 7.6 %collective-permute-start.8 = (bf16[48,640]{1,0:T(8,128)(2,1)S(1)}, bf16[48,640]{1,0:T(8,128)(2,1)S(1)}, u32[]{:S(2)}, u32[]{:S(2)}) collective-permute-start(bf16[48,640]{1,0:T(8,128)(2,1)S(1)} %get-tuple-element.142), channel_id=1, source_target_pairs={{0,16},{4,20},{8,24},{12,28},{16,0},{20,4},{24,8},{28,12},{32,48},... | collective-permute-start | bytes 184328 | tf_op jit(solution)/shard_map/ppermute | solution.py:514
  32.9 27.1 %collective-permute-start.2 = (bf16[384,768]{1,0:T(8,128)(2,1)S(1)}, bf16[384,768]{1,0:T(8,128)(2,1)S(1)}, u32[]{:S(2)}, u32[]{:S(2)}) collective-permute-start(bf16[384,768]{1,0:T(8,128)(2,1)S(1)} %copy-done.3), channel_id=1, source_target_pairs={{0,3},{1,0},{2,1},{3,2},{4,7},{5,4},{6,5},{7,6},{8,11},{9,8},{10,9... | collective-permute-start | bytes 1769480 | tf_op jit(solution)/shard_map/ppermute | solution.py:506
  33.5 26.5 %collective-permute-start.1 = (bf16[384,768]{1,0:T(8,128)(2,1)S(1)}, bf16[384,768]{1,0:T(8,128)(2,1)S(1)}, u32[]{:S(2)}, u32[]{:S(2)}) collective-permute-start(bf16[384,768]{1,0:T(8,128)(2,1)S(1)} %copy-done.3), channel_id=1, source_target_pairs={{0,2},{1,3},{2,0},{3,1},{4,6},{5,7},{6,4},{7,5},{8,10},{9,11},{10,... | collective-permute-start | bytes 1769480 | tf_op jit(solution)/shard_map/ppermute | solution.py:506
  34.1 27.8 %collective-permute-start = (bf16[384,768]{1,0:T(8,128)(2,1)S(1)}, bf16[384,768]{1,0:T(8,128)(2,1)S(1)}, u32[]{:S(2)}, u32[]{:S(2)}) collective-permute-start(bf16[384,768]{1,0:T(8,128)(2,1)S(1)} %copy-done.3), channel_id=1, source_target_pairs={{0,1},{1,2},{2,3},{3,0},{4,5},{5,6},{6,7},{7,4},{8,9},{9,10},{10,1... | collective-permute-start | bytes 1769480 | tf_op jit(solution)/shard_map/ppermute | solution.py:506
  35.1 16.8 %collective-permute-start.12 = (bf16[4,48,640]{2,1,0:T(8,128)(2,1)S(1)}, bf16[4,48,640]{2,1,0:T(8,128)(2,1)S(1)}, u32[]{:S(2)}, u32[]{:S(2)}) collective-permute-start(bf16[4,48,640]{2,1,0:T(8,128)(2,1)S(1)} %pad_maximum_fusion.2.refs_5_), channel_id=1, source_target_pairs={{0,96},{4,100},{8,104},{12,108},{16,112},{20,116},{24,120},{28,124... | collective-permute-start | bytes 737288 | tf_op jit(solution)/shard_map/ppermute | solution.py:514
  40.0 13.1 %collective-permute-start.11 = (bf16[4,48,640]{2,1,0:T(8,128)(2,1)S(1)}, bf16[4,48,640]{2,1,0:T(8,128)(2,1)S(1)}, u32[]{:S(2)}, u32[]{:S(2)}) collective-permute-start(bf16[4,48,640]{2,1,0:T(8,128)(2,1)S(1)} %pad_maximum_fusion.2.refs_5_), channel_id=1, source_target_pairs={{0,64},{4,68},{8,72},{12,76},{16,80},{20,84},{24,88},{28,92},{32,9... | collective-permute-start | bytes 737288 | tf_op jit(solution)/shard_map/ppermute | solution.py:514
  52.0 8.0 %collective-permute-start.10 = (bf16[4,48,640]{2,1,0:T(8,128)(2,1)S(1)}, bf16[4,48,640]{2,1,0:T(8,128)(2,1)S(1)}, u32[]{:S(2)}, u32[]{:S(2)}) collective-permute-start(bf16[4,48,640]{2,1,0:T(8,128)(2,1)S(1)} %pad_maximum_fusion.2.refs_5_), channel_id=1, source_target_pairs={{0,32},{4,36},{8,40},{12,44},{16,48},{20,52},{24,56},{28,60},{32,6... | collective-permute-start | bytes 737288 | tf_op jit(solution)/shard_map/ppermute | solution.py:514
  82.7 12.5 %collective-permute-start.13 = (bf16[384,192]{1,0:T(8,128)(2,1)}, bf16[384,192]{1,0:T(8,128)(2,1)S(1)}, u32[]{:S(2)}, u32[]{:S(2)}) collective-permute-start(bf16[384,192]{1,0:T(8,128)(2,1)} %get-tuple-element.66), channel_id=1, source_target_pairs={{0,1},{1,2},{2,3},{3,0},{4,5},{5,6},{6,7},{7,4},{8,9},{9,10},{10,1... | collective-permute-start | bytes 442376 | tf_op jit(solution)/shard_map/ppermute | solution.py:506
  83.6 11.6 %collective-permute-start.14 = (bf16[384,192]{1,0:T(8,128)(2,1)}, bf16[384,192]{1,0:T(8,128)(2,1)S(1)}, u32[]{:S(2)}, u32[]{:S(2)}) collective-permute-start(bf16[384,192]{1,0:T(8,128)(2,1)} %get-tuple-element.67), channel_id=1, source_target_pairs={{0,2},{1,3},{2,0},{3,1},{4,6},{5,7},{6,4},{7,5},{8,10},{9,11},{10,... | collective-permute-start | bytes 442376 | tf_op jit(solution)/shard_map/ppermute | solution.py:506
  86.4 9.7 %collective-permute-start.15 = (bf16[384,192]{1,0:T(8,128)(2,1)}, bf16[384,192]{1,0:T(8,128)(2,1)S(1)}, u32[]{:S(2)}, u32[]{:S(2)}) collective-permute-start(bf16[384,192]{1,0:T(8,128)(2,1)} %get-tuple-element.68), channel_id=1, source_target_pairs={{0,3},{1,0},{2,1},{3,2},{4,7},{5,4},{6,5},{7,6},{8,11},{9,8},{10,9... | collective-permute-start | bytes 442376 | tf_op jit(solution)/shard_map/ppermute | solution.py:506
  131.6 7.3 %collective-permute-start.16 = (bf16[384,192]{1,0:T(8,128)(2,1)S(1)}, bf16[384,192]{1,0:T(8,128)(2,1)S(1)}, u32[]{:S(2)}, u32[]{:S(2)}) collective-permute-start(bf16[384,192]{1,0:T(8,128)(2,1)S(1)} %copy-done.25), channel_id=1, source_target_pairs={{0,1},{1,2},{2,3},{3,0},{4,5},{5,6},{6,7},{7,4},{8,9},{9,10},{10,1... | collective-permute-start | bytes 442376 | tf_op jit(solution)/shard_map/ppermute | solution.py:506
  131.9 12.2 %collective-permute-start.17 = (bf16[384,192]{1,0:T(8,128)(2,1)S(1)}, bf16[384,192]{1,0:T(8,128)(2,1)S(1)}, u32[]{:S(2)}, u32[]{:S(2)}) collective-permute-start(bf16[384,192]{1,0:T(8,128)(2,1)S(1)} %copy-done.22), channel_id=1, source_target_pairs={{0,2},{1,3},{2,0},{3,1},{4,6},{5,7},{6,4},{7,5},{8,10},{9,11},{10,... | collective-permute-start | bytes 442376 | tf_op jit(solution)/shard_map/ppermute | solution.py:506
  135.5 8.6 %collective-permute-start.18 = (bf16[384,192]{1,0:T(8,128)(2,1)S(1)}, bf16[384,192]{1,0:T(8,128)(2,1)S(1)}, u32[]{:S(2)}, u32[]{:S(2)}) collective-permute-start(bf16[384,192]{1,0:T(8,128)(2,1)S(1)} %copy-done.20), channel_id=1, source_target_pairs={{0,3},{1,0},{2,1},{3,2},{4,7},{5,4},{6,5},{7,6},{8,11},{9,8},{10,9... | collective-permute-start | bytes 442376 | tf_op jit(solution)/shard_map/ppermute | solution.py:506
  173.5 17.3 %collective-permute-start.23 = (bf16[384,768]{1,0:T(8,128)(2,1)}, bf16[384,768]{1,0:T(8,128)(2,1)S(1)}, u32[]{:S(2)}, u32[]{:S(2)}) collective-permute-start(bf16[384,768]{1,0:T(8,128)(2,1)} %get-tuple-element.86), channel_id=1, source_target_pairs={{0,1},{1,2},{2,3},{3,0},{4,5},{5,6},{6,7},{7,4},{8,9},{9,10},{10,1... | collective-permute-start | bytes 1769480 | tf_op jit(solution)/shard_map/ppermute | solution.py:506
  173.6 30.0 %collective-permute-start.24 = (bf16[384,768]{1,0:T(8,128)(2,1)}, bf16[384,768]{1,0:T(8,128)(2,1)S(1)}, u32[]{:S(2)}, u32[]{:S(2)}) collective-permute-start(bf16[384,768]{1,0:T(8,128)(2,1)} %get-tuple-element.87), channel_id=1, source_target_pairs={{0,2},{1,3},{2,0},{3,1},{4,6},{5,7},{6,4},{7,5},{8,10},{9,11},{10,... | collective-permute-start | bytes 1769480 | tf_op jit(solution)/shard_map/ppermute | solution.py:506
  177.1 26.8 %collective-permute-start.25 = (bf16[384,768]{1,0:T(8,128)(2,1)}, bf16[384,768]{1,0:T(8,128)(2,1)S(1)}, u32[]{:S(2)}, u32[]{:S(2)}) collective-permute-start(bf16[384,768]{1,0:T(8,128)(2,1)} %get-tuple-element.88), channel_id=1, source_target_pairs={{0,3},{1,0},{2,1},{3,2},{4,7},{5,4},{6,5},{7,6},{8,11},{9,8},{10,9... | collective-permute-start | bytes 1769480 | tf_op jit(solution)/shard_map/ppermute | solution.py:506
  179.5 24.5 %collective-permute-start.20 = (bf16[4,24,1536]{2,1,0:T(8,128)(2,1)S(1)}, bf16[4,24,1536]{2,1,0:T(8,128)(2,1)S(1)}, u32[]{:S(2)}, u32[]{:S(2)}) collective-permute-start(bf16[4,24,1536]{2,1,0:T(8,128)(2,1)S(1)} %get-tuple-element.82), channel_id=1, source_target_pairs={{0,32},{4,36},{8,40},{12,44},{16,48},{20,52},{24,56},{28,60},{32,6... | collective-permute-start | bytes 884744 | tf_op jit(solution)/shard_map/ppermute | solution.py:514
  182.1 29.8 %collective-permute-start.21 = (bf16[4,24,1536]{2,1,0:T(8,128)(2,1)S(1)}, bf16[4,24,1536]{2,1,0:T(8,128)(2,1)S(1)}, u32[]{:S(2)}, u32[]{:S(2)}) collective-permute-start(bf16[4,24,1536]{2,1,0:T(8,128)(2,1)S(1)} %get-tuple-element.83), channel_id=1, source_target_pairs={{0,64},{4,68},{8,72},{12,76},{16,80},{20,84},{24,88},{28,92},{32,9... | collective-permute-start | bytes 884744 | tf_op jit(solution)/shard_map/ppermute | solution.py:514
  190.8 21.0 %collective-permute-start.22 = (bf16[4,24,1536]{2,1,0:T(8,128)(2,1)S(1)}, bf16[4,24,1536]{2,1,0:T(8,128)(2,1)S(1)}, u32[]{:S(2)}, u32[]{:S(2)}) collective-permute-start(bf16[4,24,1536]{2,1,0:T(8,128)(2,1)S(1)} %get-tuple-element.84), channel_id=1, source_target_pairs={{0,96},{4,100},{8,104},{12,108},{16,112},{20,116},{24,120},{28,124... | collective-permute-start | bytes 884744 | tf_op jit(solution)/shard_map/ppermute | solution.py:514
  (43 other events, 438.6 us)
Sparse Core Ops, SparseCore 0:
  24.6 63.9 all-gather.1
  130.8 107.5 reduce-scatter.1
